TPU v7x, 512 devices: a whole 4x8x8 slice. The times are simulated.
512 devices in a mesh: shot: 64 (over z, x, core), chan: 8 (over y).
Axes of the slice: x: 4, y: 8, z: 8, core: 2. Of those that a mesh axis runs over, the one named last changes fastest.
Arguments:
- blended: float32 [1024, 32, 1024], P('shot', 'chan'), may hold values from -40 to 40, as said below
- estimate: bfloat16 [1024, 32, 1024], P('shot', 'chan'), may hold values from -40 to 40, as said below
- neighbour_sources: int32 [1024, 6], P('shot'), may hold values from 0 to 1023, as said below
- partner_lags: int32 [1024, 6], P('shot'), may hold values from -1023 to 1024, as said below
- threshold_level: int32 [1], replicated, may hold values from 2 to 6
Outputs:
- deblended: float32 [1024, 32, 1024], P('shot', 'chan')
Inputs may be any that keep to these rules, and one draw needn't show every extreme that they name: `neighbour_sources`: shot s is at position k of fleet g0, where (s + 1) modulo 1024 equals g0 * 512 + k. Slot 3 * g + e (e in 0, 1, 2) holds the shot at position k + e - 1 of fleet g, that is (g * 512 + k + e - 2) modulo 1024, when that position lies in 0..511, the shot is not s, and its window meets that of s; every other slot holds s itself. The relation is symmetric. `partner_lags`: A listed partner's offset is its firing time minus that of the shot, of magnitude under 1024, and the partner lists the shot with the negated offset; a slot holding the shot itself has offset 1024. `blended`: Real-valued traces. `estimate`: Real-valued traces.
All inputs are finite; a program needn't handle non-finite values.
Results may differ from a plain program's by a relative error of at most 0.02.
Values may be sent and summed in bfloat16 or wider, within the bound.
No kernel may reach another device: no remote copies, remote signals or barrier semaphores. Data moves between devices by JAX's collectives and lax.ppermute only.
A program may use at most 64 MiB of HBM per device.

v0:
```python
import functools

import jax
import jax.numpy as jnp
import numpy as np
from jax import lax
from jax.experimental import pallas as pl
from jax.experimental.pallas import tpu as pltpu
from jax.sharding import Mesh
from jax.sharding import PartitionSpec as P

SHOTS, SAMPLES, FREQS = 1024, 1024, 512
PLACES, BLOCK = 32, 16
STEP = 24
INTERPRET = False


def time_table():
    t = np.arange(SAMPLES)[:, None]
    k = np.arange(FREQS)[None, :]
    phase = 2 * np.pi * ((t * k) % SAMPLES) / SAMPLES
    both = np.stack([np.cos(phase), -np.sin(phase)], 0).reshape(2, SAMPLES, PLACES, 16)
    return (both.transpose(1, 2, 0, 3).reshape(SAMPLES, SAMPLES) / 32).astype(jnp.bfloat16)


def time_back_table():
    t = np.arange(SAMPLES)[None, :]
    k = np.arange(FREQS)[:, None]
    phase = 2 * np.pi * ((t * k) % SAMPLES) / SAMPLES
    weight = np.where(k == 0, 1.0, 2.0) / 32
    both = np.stack([weight * np.cos(phase), -weight * np.sin(phase)], 0).reshape(2, PLACES, 16, SAMPLES)
    return both.transpose(1, 0, 2, 3).reshape(SAMPLES, SAMPLES).astype(jnp.bfloat16)


def shot_table(rows):
    q = np.arange(256)[None, :]
    phase = 2 * np.pi * ((rows[:, None] * q) % 256) / 256
    return np.concatenate([np.cos(phase), np.sin(phase)], 0).astype(jnp.bfloat16)


def twiddles(rows):
    phase = 2 * np.pi * rows[:, None] * np.arange(4)[None, :] / SHOTS
    both = np.concatenate([np.repeat(np.cos(phase), 32, 1), np.repeat(np.sin(phase), 32, 1)], 1)
    return both.astype(np.float32)


def merge_table():
    out = np.zeros((2, 2, 2, 2, 16, 2, 4, 2, 16), np.float32)
    for a1 in range(2):
        for f in range(2):
            for q1 in range(4):
                turn = np.exp(-0.5j * np.pi * (2 * f + a1) * q1)
                re, im = round(turn.real), round(turn.imag)
                for c in range(2):
                    for kk in range(16):
                        out[a1, f, c, 0, kk, 0, q1, c, kk] = re
                        out[a1, f, c, 0, kk, 1, q1, c, kk] = im
                        out[a1, f, c, 1, kk, 0, q1, c, kk] = -im
                        out[a1, f, c, 1, kk, 1, q1, c, kk] = re
    return out.reshape(256, 256).astype(jnp.bfloat16)


def split_table():
    out = np.zeros((2, 2, 4, 2, 16, 4, 2, 2, 2, 16), np.float32)
    for h in range(2):
        for q1 in range(4):
            for a in range(4):
                turn = np.exp(0.5j * np.pi * a * q1)
                re, im = round(turn.real) / 32, round(turn.imag) / 32
                for c in range(2):
                    for kk in range(16):
                        out[h, 0, q1, c, kk, a, h, c, 0, kk] = re
                        out[h, 0, q1, c, kk, a, h, c, 1, kk] = im
                        out[h, 1, q1, c, kk, a, h, c, 0, kk] = -im
                        out[h, 1, q1, c, kk, a, h, c, 1, kk] = re
    return out.reshape(512, 512).astype(jnp.bfloat16)


def back_rows():
    h, jl, i = np.meshgrid(np.arange(2), np.arange(16), np.arange(8), indexing="ij")
    return (16 * jl + 8 * h + i).reshape(-1)


def lane_ids(rows):
    return lax.broadcasted_iota(jnp.int32, (rows, 128), 1)


def rolled(value, shift):
    return value if shift % 128 == 0 else pltpu.roll(value, shift % 128, 1)


def by_group(pieces, group):
    return jnp.where(
        group < 2,
        jnp.where(group == 0, pieces[0], pieces[1]),
        jnp.where(group == 2, pieces[2], pieces[3]),
    )


def blend_kernel(lag_ref, ex_ref, low_ref, high_ref, table_hbm, out_ref, est, res, dat, upd, table, sem):
    copy = pltpu.make_async_copy(table_hbm, table, sem)
    copy.start()
    place = lax.axis_index("j")
    est[...] = jnp.zeros_like(est)
    res[...] = jnp.zeros_like(res)

    def put(ref, rows, f, row, value):
        base = (f * rows + row) * 2 * STEP + 16
        ref[pl.ds(base, 8), :] = value[:8]
        ref[pl.ds(base + STEP, 8), :] = value[8:]

    at_start = jnp.where(place == 0, 1, 0)
    at_end = jnp.where(place == PLACES - 1, 1, 0)
    for f in range(2):
        low = jnp.where(at_start == 1, 1 - f, f)
        high = jnp.where(at_end == 1, 1 - f, f)
        for i in range(2):
            put(est, 20, f, i, low_ref[low, i].astype(jnp.float32))
            put(est, 20, f, 18 + i, high_ref[high, i].astype(jnp.float32))
        dat[f * 18] = low_ref[low, 2].astype(jnp.float32)
        dat[f * 18 + 17] = high_ref[high, 2].astype(jnp.float32)
        for i in range(BLOCK):
            put(est, 20, f, i + 2, ex_ref[f, i, 0].astype(jnp.float32))
            dat[f * 18 + i + 1] = ex_ref[f, i, 1].astype(jnp.float32)

    lanes = lane_ids(8)

    def companions(ref, rows, f, row, shot):
        fleet = ((shot + 1) >> 9) & 1
        own = shot * 6 + 3 * fleet
        other = shot * 6 + 3 - 3 * fleet
        total = [None, None]
        for at, side, step in ((own, 0, -1), (own + 2, 0, 1), (other, 1, -1), (other + 1, 1, 0), (other + 2, 1, 1)):
            lag = lag_ref[at]
            turn = lag & 127
            keep = lanes < 128 - turn
            first = ((f ^ side) * rows + row + step) * 2 * STEP + 16 - (lag >> 7)
            for c in range(2):
                here = ref[pl.ds(first + c * STEP, 8), :]
                before = ref[pl.ds(first + c * STEP - 1, 8), :]
                moved = pltpu.roll(jnp.where(keep, here, before), turn, 1)
                total[c] = moved if total[c] is None else total[c] + moved
        return total

    def rows_of(ref, rows, f, row):
        base = (f * rows + row) * 2 * STEP + 16
        return ref[pl.ds(base, 8), :], ref[pl.ds(base + STEP, 8), :]

    @pl.loop(0, 18)
    def _(n):
        for f in range(2):
            shot = (512 * f + BLOCK * place + n - 1 + SHOTS) & (SHOTS - 1)
            total = companions(est, 20, f, n + 1, shot)
            own = rows_of(est, 20, f, n + 1)
            data = dat[f * 18 + n]
            base = (f * 18 + n) * 2 * STEP + 16
            for c in range(2):
                value = data[8 * c : 8 * c + 8] - own[c] - total[c]
                ref_value = value.astype(jnp.bfloat16).astype(jnp.float32)
                res[pl.ds(base + c * STEP, 8), :] = ref_value

    @pl.loop(0, BLOCK)
    def _(n):
        for f in range(2):
            shot = (512 * f + BLOCK * place + n) & (SHOTS - 1)
            total = companions(res, 18, f, n + 1, shot)
            own = rows_of(est, 20, f, n + 2)
            left = rows_of(res, 18, f, n + 1)
            for c in range(2):
                value = own[c] + 0.25 * (left[c] + total[c])
                upd[pl.ds(((f * 2 + c) * BLOCK + n) * 8, 8), :] = value

    parts = [upd[pl.ds(u, 64, stride=8), :] for u in range(8)]
    lhs = jnp.concatenate(parts, 1).astype(jnp.bfloat16)
    copy.wait()
    group = lane_ids(BLOCK) // 32
    for half in range(4):
        product = jnp.dot(lhs, table[:, 256 * half : 256 * half + 256], preferred_element_type=jnp.float32)
        for m in range(2):
            block = product[:, 128 * m : 128 * m + 128]
            turned = [[rolled(block[16 * g : 16 * g + 16], 32 * k) for k in range(4)] for g in range(4)]
            for d in range(4):
                chunk = by_group([turned[g][(g - d) % 4] for g in range(4)], group)
                out_ref[8 * half + 4 * m + d] = chunk.astype(jnp.bfloat16)


def forward_kernel(x_ref, merge_ref, turn_ref, shots_ref, spec_ref, peak_ref):
    lhs = jnp.concatenate([x_ref[:256], x_ref[256:]], 1)
    merged = jnp.dot(lhs, merge_ref[...], preferred_element_type=jnp.float32)
    re, im = merged[:, :128], merged[:, 128:]
    cos, sin = turn_ref[:, :128], turn_ref[:, 128:]
    rhs = jnp.concatenate([re * cos + im * sin, im * cos - re * sin], 1).astype(jnp.bfloat16)
    product = jnp.dot(shots_ref[...], rhs, preferred_element_type=jnp.float32) * (1 / 32)
    re = product[:256, :128] + product[256:, 128:]
    im = product[:256, 128:] - product[256:, :128]
    spec_ref[:, :128] = re
    spec_ref[:, 128:] = im
    peak = jnp.max(re * re + im * im, axis=0, keepdims=True)
    peak = jnp.broadcast_to(peak, (8, 128))
    for shift in (16, 32, 64):
        peak = jnp.maximum(peak, pltpu.roll(peak, shift, 1))
    peak_ref[...] = jnp.broadcast_to(peak[None], peak_ref.shape)


def backward_kernel(level_ref, spec_ref, peak_ref, shots_ref, turn_ref, split_ref, out_ref):
    peak = jnp.sqrt(jnp.max(peak_ref[...].reshape(-1, 128), axis=0, keepdims=True))
    limit = level_ref[0].astype(jnp.float32) * (1 / 64) * (peak + 1e-6)
    re, im = spec_ref[:, :128], spec_ref[:, 128:]
    size = jnp.sqrt(re * re + im * im)
    factor = jnp.maximum(size - limit, 0.0) / jnp.maximum(size, limit)
    rhs = jnp.concatenate([re * factor, im * factor], 1).astype(jnp.bfloat16)
    product = jnp.dot(shots_ref[...], rhs, preferred_element_type=jnp.float32)
    re = product[:256, :128] - product[256:, 128:]
    im = product[:256, 128:] + product[256:, :128]
    cos, sin = turn_ref[:, :128], turn_ref[:, 128:]
    turned = jnp.concatenate([re * cos - im * sin, im * cos + re * sin], 1).astype(jnp.bfloat16)
    lhs = jnp.concatenate([turned[:128], turned[128:]], 1)
    product = jnp.dot(lhs, split_ref[...], preferred_element_type=jnp.float32)
    for a in range(4):
        out_ref[128 * a : 128 * a + 128] = product[:, 128 * a : 128 * a + 128].astype(jnp.bfloat16)


def time_back_kernel(x_ref, table_ref, out_ref, lhs):
    x = x_ref[...].astype(jnp.float32)
    group = lane_ids(8) // 32
    for zh in range(2):
        for m in range(8):
            tiles = [x[(zh * 32 + 4 * m + d) * 8 :][:8] for d in range(4)]
            turned = [[rolled(tiles[d], 32 * k) for k in range(4)] for d in range(4)]
            for g in range(4):
                piece = by_group([turned[d][(d - g) % 4] for d in range(4)], group)
                lhs[(zh * 4 + g) * 8 : (zh * 4 + g) * 8 + 8, 128 * m : 128 * m + 128] = piece
    left = lhs[...].astype(jnp.bfloat16)
    for n in range(4):
        columns = slice(256 * n, 256 * n + 256)
        product = jnp.dot(left, table_ref[:, columns], preferred_element_type=jnp.float32)
        for zh in range(2):
            for h in range(2):
                for c in range(2):
                    row = (zh * 4 + 2 * h + c) * 8
                    out_ref[8 * h : 8 * h + 8, 2 * zh + c, columns] = product[row : row + 8]


def vmem(count):
    return [pl.BlockSpec(memory_space=pltpu.VMEM)] * count


def smem():
    return pl.BlockSpec(memory_space=pltpu.SMEM)


PARAMS = pltpu.CompilerParams(vmem_limit_bytes=32 * 1024 * 1024)


def call(kernel, outs, in_specs, scratch=(), out_count=1):
    return pl.pallas_call(
        kernel,
        out_shape=outs,
        in_specs=in_specs,
        out_specs=vmem(out_count) if out_count > 1 else vmem(1)[0],
        scratch_shapes=list(scratch),
        compiler_params=PARAMS,
        interpret=INTERPRET,
    )


def local(blended, estimate, neighbour_sources, partner_lags, threshold_level):
    lags = lax.all_gather(partner_lags.reshape(-1), ("zh", "j"), axis=0, tiled=True)
    both = jnp.stack([estimate, blended.astype(jnp.bfloat16)], 1)
    both = both.reshape(BLOCK, 2, 2, 16, 128).transpose(2, 0, 1, 3, 4)
    ex = lax.all_to_all(both, "zh", 0, 0, tiled=True)
    up = jnp.concatenate([ex[:, 14:, 0], ex[:, 15:, 1]], 1)
    down = jnp.concatenate([ex[:, :2, 0], ex[:, :1, 1]], 1)
    low = lax.ppermute(up, "j", [(i, (i + 1) % PLACES) for i in range(PLACES)])
    high = lax.ppermute(down, "j", [((i + 1) % PLACES, i) for i in range(PLACES)])
    send = call(
        blend_kernel,
        jax.ShapeDtypeStruct((PLACES, BLOCK, 128), jnp.bfloat16),
        [smem()] + vmem(3) + [pl.BlockSpec(memory_space=pl.ANY)],
        [
            pltpu.VMEM((80 * STEP + 16, 128), jnp.float32),
            pltpu.VMEM((72 * STEP + 16, 128), jnp.float32),
            pltpu.VMEM((36, 16, 128), jnp.float32),
            pltpu.VMEM((512, 128), jnp.float32),
            pltpu.VMEM((SAMPLES, SAMPLES), jnp.bfloat16),
            pltpu.SemaphoreType.DMA,
        ],
    )(lags, ex, low, high, time_table())
    columns = lax.all_to_all(send, "j", 0, 0, tiled=True).reshape(512, 128)
    others = lax.axis_size("zh") * lax.axis_size("chan")
    spec, peak = call(
        forward_kernel,
        (jax.ShapeDtypeStruct((256, 256), jnp.float32), jax.ShapeDtypeStruct((others, 8, 128), jnp.float32)),
        vmem(4),
        out_count=2,
    )(columns, merge_table(), twiddles(np.arange(256)), shot_table(np.arange(256)))
    peaks = lax.all_to_all(peak, ("zh", "chan"), 0, 0, tiled=True)
    rows = back_rows()
    back = call(
        backward_kernel,
        jax.ShapeDtypeStruct((512, 128), jnp.bfloat16),
        [smem()] + vmem(5),
    )(threshold_level, spec, peaks, shot_table(rows), twiddles(rows), split_table())
    arrived = lax.all_to_all(back.reshape(64, 8, 128), ("zh", "j"), 0, 0, tiled=True).reshape(512, 128)
    return call(
        time_back_kernel,
        jax.ShapeDtypeStruct((BLOCK, 4, SAMPLES), jnp.float32),
        vmem(2),
        [pltpu.VMEM((64, SAMPLES), jnp.float32)],
    )(arrived, time_back_table())


def solution(mesh):
    split = Mesh(mesh.devices.reshape(2, PLACES, -1), ("zh", "j", "chan"))
    shots = P(("zh", "j"), "chan", None)
    return jax.shard_map(
        local,
        mesh=split,
        in_specs=(shots, shots, P(("zh", "j"), None), P(("zh", "j"), None), P()),
        out_specs=shots,
        check_vma=False,
    )
```

profile of v0, /device:TPU:1, one launch (start us, length us, event | category | flops | bytes accessed | tf_op | source)
XLA Modules:
  0.0 350.2 jit_solution(14410602017690721889)
XLA Ops:
  0.0 0.0 copy-start.1
  0.0 1.1 convert_element_type.3
  1.2 0.1 stack.10
  1.2 1.0 stack.9
  2.2 0.0 copy-start.3
  2.2 0.0 copy-start.4
  2.2 0.0 copy-start.9
  2.3 19.1 %all_to_all.20.ex_ref = bf16[2,16,2,16,128]{4,3,2,1,0:T(8,128)(2,1)S(1)} all-to-all(bf16[2,16,2,16,128]{4,3,2,1,0:T(8,128)(2,1)S(1)} %copy.27), channel_id=1, replica_groups=mesh['zh'=2,'j'=32,'chan'=8] {'zh'}, dimensions={0} | all-to-all | bytes 524288 | tf_op jit(solution)/shard_map/all_to_all | solution.py:271
  21.4 0.0 copy-start.2
  21.4 0.6 pad_maximum_fusion.1
  22.0 6.4 %collective-permute-start.1 = (bf16[2,3,16,128]{3,2,1,0:T(8,128)(2,1)}, bf16[2,3,16,128]{3,2,1,0:T(8,128)(2,1)}, u32[]{:S(2)}, u32[]{:S(2)}) collective-permute-start(bf16[2,3,16,128]{3,2,1,0:T(8,128)(2,1)} %pad_maximum_fusion.1), channel_id=1, source_target_pairs={{8,0},{16,8},{24,16},{32,24},{40,32},{48,40},{56,48},{64,56},{72,6... | collective-permute-start | bytes 73736 | tf_op jit(solution)/shard_map/ppermute | solution.py:275
  28.4 0.6 pad_maximum_fusion
  29.0 3.0 collective-permute-start
  32.0 0.8 copy.26
  32.8 0.1 reshape.21
  32.9 1.3 dynamic-slice
  34.8 0.6 broadcast
  35.4 1.4 dynamic-update-slice
  36.9 243.2 %all-reduce.lag_ref = s32[6144]{0:T(1024)} all-reduce(s32[6144]{0:T(1024)} %dynamic-update-slice), channel_id=1, replica_groups=mesh['zh'=2,'j'=32,'chan'=8] {'zh','j'}, use_global_device_ids=true, to_apply=%add | all-reduce | flops 6144 | bytes 49152
  280.1 0.0 collective-permute-done.1.high_ref
  280.1 0.0 collective-permute-done.low_ref
  280.1 0.0 copy-done.1
  280.1 0.0 copy-start.10
  280.1 0.7 copy-done.10
  280.9 5.1 %shard_map.118 = bf16[32,16,128]{2,1,0:T(8,128)(2,1)S(1)} custom-call(s32[6144]{0:T(1024)S(1)} %copy-done.10, bf16[2,16,2,16,128]{4,3,2,1,0:T(8,128)(2,1)S(1)} %all_to_all.20.ex_ref, bf16[2,3,16,128]{3,2,1,0:T(8,128)(2,1)} %collective-permute-done.low_ref, bf16[2,3,16,128]{3,2,1,0:T(8,128)(2,1)} %collective-permute-done.1.high_ref, ...), custom_call_target="tpu_custom_call" | custom-call | tf_op jit(solution)/shard_map/pallas_call | solution.py:276
  286.0 0.0 copy-start
  286.0 18.8 %all_to_all.21 = bf16[32,16,128]{2,1,0:T(8,128)(2,1)S(1)} all-to-all(bf16[32,16,128]{2,1,0:T(8,128)(2,1)S(1)} %shard_map.118), channel_id=1, replica_groups=mesh['zh'=2,'j'=32,'chan'=8] {'j'}, dimensions={0} | all-to-all | bytes 262144 | tf_op jit(solution)/shard_map/all_to_all | solution.py:289
  304.8 0.0 copy-done.3
  304.8 0.0 copy-done.4
  304.8 0.0 copy-done.9
  304.8 1.3 shard_map.119
  306.1 0.0 copy-start.7
  306.1 0.7 copy-done.7
  306.8 11.1 %all-to-all-start.2 = ((f32[16,8,128]{2,1,0:T(8,128)}), f32[16,8,128]{2,1,0:T(8,128)S(1)}, u32[]{:S(2)}, u32[]{:S(2)}) async-start(f32[16,8,128]{2,1,0:T(8,128)} %get-tuple-element.8), calls=%async_computation.2 | async-start | bytes 131072 | tf_op jit(solution)/shard_map/all_to_all | solution.py:297
  318.5 10.6 %all-to-all-done.2.peak_ref = f32[16,8,128]{2,1,0:T(8,128)S(1)} async-done(((f32[16,8,128]{2,1,0:T(8,128)}), f32[16,8,128]{2,1,0:T(8,128)S(1)}, u32[]{:S(2)}, u32[]{:S(2)}) %all-to-all-start.2) | async-done | bytes 65568 | tf_op jit(solution)/shard_map/all_to_all | solution.py:297
  329.1 0.0 copy-done.2
  329.1 0.0 copy-start.5
  329.1 0.9 copy-done.5
  330.1 0.0 copy-start.6
  330.1 0.9 copy-done.6
  331.0 0.0 copy-start.8
  331.1 0.9 copy-done.8
  332.0 0.5 shard_map.120
  332.5 16.4 %all_to_all.22 = bf16[64,8,128]{2,1,0:T(8,128)(2,1)S(1)} all-to-all(bf16[64,8,128]{2,1,0:T(8,128)(2,1)S(1)} %bitcast.24), channel_id=1, replica_groups=mesh['zh'=2,'j'=32,'chan'=8] {'zh','j'}, dimensions={0} | all-to-all | bytes 262144 | tf_op jit(solution)/shard_map/all_to_all | solution.py:304
  349.0 0.0 copy-done
  349.0 1.3 shard_map.121
  (4 shorter events, 0.1 us)
Async XLA Ops:
  0.0 280.1 %copy-start.1 = (bf16[1024,1024]{1,0:T(8,128)(2,1)S(1)}, bf16[1024,1024]{1,0:T(8,128)(2,1)}, u32[]{:S(2)}) copy-start(bf16[1024,1024]{1,0:T(8,128)(2,1)} %constant.16.clone.table_hbm) | copy-start | bytes 6291460
  2.2 302.6 %copy-start.3 = (f32[256,256]{1,0:T(8,128)S(1)}, f32[256,256]{1,0:T(8,128)}, u32[]{:S(2)}) copy-start(f32[256,256]{1,0:T(8,128)} %constant.18.clone.turn_ref) | copy-start | bytes 786436
  2.2 302.6 %copy-start.4 = (bf16[512,256]{1,0:T(8,128)(2,1)S(1)}, bf16[512,256]{1,0:T(8,128)(2,1)}, u32[]{:S(2)}) copy-start(bf16[512,256]{1,0:T(8,128)(2,1)} %constant.19.clone.shots_ref) | copy-start | bytes 786436
  2.2 302.6 %copy-start.9 = (bf16[256,256]{1,0:T(8,128)(2,1)S(1)}, bf16[256,256]{1,0:T(8,128)(2,1)}, u32[]{:S(2)}) copy-start(bf16[256,256]{1,0:T(8,128)(2,1)} %constant.17.clone.merge_ref) | copy-start | bytes 393220
  21.4 307.8 %copy-start.2 = (bf16[512,512]{1,0:T(8,128)(2,1)S(1)}, bf16[512,512]{1,0:T(8,128)(2,1)}, u32[]{:S(2)}) copy-start(bf16[512,512]{1,0:T(8,128)(2,1)} %constant.22.clone.split_ref) | copy-start | bytes 1572868
  22.0 258.1 %collective-permute-start.1 = (bf16[2,3,16,128]{3,2,1,0:T(8,128)(2,1)}, bf16[2,3,16,128]{3,2,1,0:T(8,128)(2,1)}, u32[]{:S(2)}, u32[]{:S(2)}) collective-permute-start(bf16[2,3,16,128]{3,2,1,0:T(8,128)(2,1)} %pad_maximum_fusion.1), channel_id=1, source_target_pairs={{8,0},{16,8},{24,16},{32,24},{40,32},{48,40},{56,48},{64,56},{72,6... | collective-permute-start | bytes 73736 | tf_op jit(solution)/shard_map/ppermute | solution.py:275
  29.0 251.1 %collective-permute-start = (bf16[2,3,16,128]{3,2,1,0:T(8,128)(2,1)}, bf16[2,3,16,128]{3,2,1,0:T(8,128)(2,1)}, u32[]{:S(2)}, u32[]{:S(2)}) collective-permute-start(bf16[2,3,16,128]{3,2,1,0:T(8,128)(2,1)} %pad_maximum_fusion), channel_id=1, source_target_pairs={{0,8},{8,16},{16,24},{24,32},{32,40},{40,48},{48,56},{56,64},{64,7... | collective-permute-start | bytes 73736 | tf_op jit(solution)/shard_map/ppermute | solution.py:274
  280.1 0.7 copy-start.10
  286.0 63.0 %copy-start = (bf16[1024,1024]{1,0:T(8,128)(2,1)S(1)}, bf16[1024,1024]{1,0:T(8,128)(2,1)}, u32[]{:S(2)}) copy-start(bf16[1024,1024]{1,0:T(8,128)(2,1)} %constant.23.clone.table_ref) | copy-start | bytes 6291460
  306.1 0.7 copy-start.7
  306.8 22.4 %all-to-all-start.2 = ((f32[16,8,128]{2,1,0:T(8,128)}), f32[16,8,128]{2,1,0:T(8,128)S(1)}, u32[]{:S(2)}, u32[]{:S(2)}) async-start(f32[16,8,128]{2,1,0:T(8,128)} %get-tuple-element.8), calls=%async_computation.2 | async-start | bytes 131072 | tf_op jit(solution)/shard_map/all_to_all | solution.py:297
  329.1 1.0 copy-start.5
  330.1 0.9 copy-start.6
  331.0 0.9 copy-start.8
where the time goes:
time: 351 us; the launch traced here: 350 us
  blocking collectives  298 us (85%)
  starting transfers between devices  20.5 us (6%)
  waiting for transfers between devices  10.6 us (3%)
  local copies, waits for them, and re-layouts  9.54 us (3%)
  Pallas kernels  8.2 us (2%)
    unnamed x1, blocking collectives  243 us
    all_to_all x1, blocking collectives, local(): ex = lax.all_to_all(both, 'zh', 0, 0, tiled=True)  19.1 us
    all_to_all x1, blocking collectives, local(): columns = lax.all_to_all(send, 'j', 0, 0, tiled=True).reshape(512, 128)  18.8 us
    all_to_all x1, blocking collectives, local(): lax.all_to_all(back.reshape(64, 8, 128), ('zh', 'j'), 0, 0, tiled=True)  16.4 us
    all_to_all x1, starting transfers between devices, local(): peaks = lax.all_to_all(peak, ('zh', 'chan'), 0, 0, tiled=True)  11.1 us
    all_to_all x1, waiting for transfers between devices, local(): peaks = lax.all_to_all(peak, ('zh', 'chan'), 0, 0, tiled=True)  10.6 us
    unnamed x26, local copies, waits for them, and re-layouts  8.41 us
  transfers between devices with their start and end apart: 3, of which 1 were waited for; matrix products, arithmetic and copies ran while one was open for 1% of the time, Pallas kernels for 0%

commit v1 on v0

--- a/solution.py
+++ b/solution.py
@@ -97,7 +97,9 @@
     )
 
 
-def blend_kernel(lag_ref, ex_ref, low_ref, high_ref, table_hbm, out_ref, est, res, dat, upd, table, sem):
+def blend_kernel(
+    ex_ref, low_ref, high_ref, table_hbm, out_ref, est, res, dat, upd, table, lag_vmem, lag_ref, sem, lag_sem
+):
     copy = pltpu.make_async_copy(table_hbm, table, sem)
     copy.start()
     place = lax.axis_index("j")
@@ -111,6 +113,13 @@
 
     at_start = jnp.where(place == 0, 1, 0)
     at_end = jnp.where(place == PLACES - 1, 1, 0)
+    for f in range(2):
+        low = jnp.where(at_start == 1, 1 - f, f)
+        high = jnp.where(at_end == 1, 1 - f, f)
+        coded = jnp.concatenate([r.astype(jnp.float32) for r in (low_ref[low, 3], ex_ref[f, 32], high_ref[high, 3])], 0)
+        lag_vmem[f] = (32.0 * coded + pltpu.roll(coded, 120, 1)).astype(jnp.int32)
+    lag_copy = pltpu.make_async_copy(lag_vmem, lag_ref, lag_sem)
+    lag_copy.start()
     for f in range(2):
         low = jnp.where(at_start == 1, 1 - f, f)
         high = jnp.where(at_end == 1, 1 - f, f)
@@ -120,18 +129,19 @@
         dat[f * 18] = low_ref[low, 2].astype(jnp.float32)
         dat[f * 18 + 17] = high_ref[high, 2].astype(jnp.float32)
         for i in range(BLOCK):
-            put(est, 20, f, i + 2, ex_ref[f, i, 0].astype(jnp.float32))
-            dat[f * 18 + i + 1] = ex_ref[f, i, 1].astype(jnp.float32)
-
+            put(est, 20, f, i + 2, ex_ref[f, i].astype(jnp.float32))
+            dat[f * 18 + i + 1] = ex_ref[f, BLOCK + i].astype(jnp.float32)
+
+    lag_copy.wait()
     lanes = lane_ids(8)
 
-    def companions(ref, rows, f, row, shot):
-        fleet = ((shot + 1) >> 9) & 1
-        own = shot * 6 + 3 * fleet
-        other = shot * 6 + 3 - 3 * fleet
+    def companions(ref, rows, f, row, n):
+        fleet = ((512 * f + BLOCK * place + n + SHOTS + 1) >> 9) & 1
+        own = 3 * fleet
+        other = 3 - 3 * fleet
         total = [None, None]
         for at, side, step in ((own, 0, -1), (own + 2, 0, 1), (other, 1, -1), (other + 1, 1, 0), (other + 2, 1, 1)):
-            lag = lag_ref[at]
+            lag = lag_ref[f, BLOCK + n, at]
             turn = lag & 127
             keep = lanes < 128 - turn
             first = ((f ^ side) * rows + row + step) * 2 * STEP + 16 - (lag >> 7)
@@ -149,8 +159,7 @@
     @pl.loop(0, 18)
     def _(n):
         for f in range(2):
-            shot = (512 * f + BLOCK * place + n - 1 + SHOTS) & (SHOTS - 1)
-            total = companions(est, 20, f, n + 1, shot)
+            total = companions(est, 20, f, n + 1, n - 1)
             own = rows_of(est, 20, f, n + 1)
             data = dat[f * 18 + n]
             base = (f * 18 + n) * 2 * STEP + 16
@@ -162,8 +171,7 @@
     @pl.loop(0, BLOCK)
     def _(n):
         for f in range(2):
-            shot = (512 * f + BLOCK * place + n) & (SHOTS - 1)
-            total = companions(res, 18, f, n + 1, shot)
+            total = companions(res, 18, f, n + 1, n)
             own = rows_of(est, 20, f, n + 2)
             left = rows_of(res, 18, f, n + 1)
             for c in range(2):
@@ -265,27 +273,32 @@
 
 
 def local(blended, estimate, neighbour_sources, partner_lags, threshold_level):
-    lags = lax.all_gather(partner_lags.reshape(-1), ("zh", "j"), axis=0, tiled=True)
-    both = jnp.stack([estimate, blended.astype(jnp.bfloat16)], 1)
-    both = both.reshape(BLOCK, 2, 2, 16, 128).transpose(2, 0, 1, 3, 4)
+    est = estimate.reshape(BLOCK, 2, 16, 128)
+    data = blended.astype(jnp.bfloat16).reshape(BLOCK, 2, 16, 128)
+    lags = jnp.pad(jnp.concatenate([jnp.pad(partner_lags >> 5, ((0, 0), (0, 2))), partner_lags & 31], 1), ((0, 0), (0, 114)))
+    lags = jnp.broadcast_to(lags.astype(jnp.bfloat16)[None, None], (1, 2, 16, 128))
+    both = jnp.concatenate([est, data, lags], 0).transpose(1, 0, 2, 3)
     ex = lax.all_to_all(both, "zh", 0, 0, tiled=True)
-    up = jnp.concatenate([ex[:, 14:, 0], ex[:, 15:, 1]], 1)
-    down = jnp.concatenate([ex[:, :2, 0], ex[:, :1, 1]], 1)
+    up = jnp.concatenate([ex[:, 14:16], ex[:, 31:33]], 1)
+    down = jnp.concatenate([ex[:, :2], ex[:, 16:17], ex[:, 32:]], 1)
     low = lax.ppermute(up, "j", [(i, (i + 1) % PLACES) for i in range(PLACES)])
     high = lax.ppermute(down, "j", [((i + 1) % PLACES, i) for i in range(PLACES)])
     send = call(
         blend_kernel,
         jax.ShapeDtypeStruct((PLACES, BLOCK, 128), jnp.bfloat16),
-        [smem()] + vmem(3) + [pl.BlockSpec(memory_space=pl.ANY)],
+        vmem(3) + [pl.BlockSpec(memory_space=pl.ANY)],
         [
             pltpu.VMEM((80 * STEP + 16, 128), jnp.float32),
             pltpu.VMEM((72 * STEP + 16, 128), jnp.float32),
             pltpu.VMEM((36, 16, 128), jnp.float32),
             pltpu.VMEM((512, 128), jnp.float32),
             pltpu.VMEM((SAMPLES, SAMPLES), jnp.bfloat16),
+            pltpu.VMEM((2, 48, 128), jnp.int32),
+            pltpu.SMEM((2, 48, 128), jnp.int32),
+            pltpu.SemaphoreType.DMA,
             pltpu.SemaphoreType.DMA,
         ],
-    )(lags, ex, low, high, time_table())
+    )(ex, low, high, time_table())
     columns = lax.all_to_all(send, "j", 0, 0, tiled=True).reshape(512, 128)
     others = lax.axis_size("zh") * lax.axis_size("chan")
     spec, peak = call(

time: 351 us -> 95.7 us (0.27)
  blocking collectives: 298 us -> 54.4 us
  local copies, waits for them, and re-layouts: 9.54 us -> 1.18 us
  starting transfers between devices: 20.5 us -> 16.6 us
    unnamed x1 -> x0, blocking collectives: 243 us -> none
    unnamed x26 -> x17, local copies, waits for them, and re-layouts: 8.41 us -> 0.14 us
    all_to_all x1, starting transfers between devices: 11.1 us -> 6.93 us  [local(): peaks = lax.all_to_all(peak, ('zh', 'chan'), 0, 0, tiled=True)]
  transfers between devices with their start and end apart: 3 -> 3, of which waited for: 1 -> 2; matrix products, arithmetic and copies ran while one was open for 1% -> 0% of each run, Pallas kernels for 0% -> 0%
where the time goes in v1:
time: 95.7 us; the launch traced here: 95.3 us
  blocking collectives  54.4 us (57%)
  starting transfers between devices  16.6 us (17%)
  waiting for transfers between devices  11.6 us (12%)
  Pallas kernels  8.84 us (9%)
  other arithmetic  1.88 us (2%)
  local copies, waits for them, and re-layouts  1.18 us (1%)
    all_to_all x1, blocking collectives, local(): ex = lax.all_to_all(both, 'zh', 0, 0, tiled=True)  19.2 us
    all_to_all x1, blocking collectives, local(): columns = lax.all_to_all(send, 'j', 0, 0, tiled=True).reshape(512, 128)  18.7 us
    all_to_all x1, blocking collectives, local(): lax.all_to_all(back.reshape(64, 8, 128), ('zh', 'j'), 0, 0, tiled=True)  16.5 us
    all_to_all x1, waiting for transfers between devices, local(): peaks = lax.all_to_all(peak, ('zh', 'chan'), 0, 0, tiled=True)  10.6 us
    all_to_all x1, starting transfers between devices, local(): peaks = lax.all_to_all(peak, ('zh', 'chan'), 0, 0, tiled=True)  6.93 us
    ppermute x1, starting transfers between devices, local(): lax.ppermute(down, 'j', [((i + 1) % PLACES, i) for i in range(PLACES)])  6.65 us
    pallas_call x1, Pallas kernels, local(): call(blend_kernel, jax.ShapeDtypeStruct((PLACES, BLOCK, 128), jnp.bfloat1...  5.75 us
    ppermute x1, starting transfers between devices, local(): low = lax.ppermute(up, 'j', [(i, (i + 1) % PLACES) for i in range(PLACES)])  3.02 us
  transfers between devices with their start and end apart: 3, of which 2 were waited for; matrix products, arithmetic and copies ran while one was open for 0% of the time, Pallas kernels for 0%

profile of v1, /device:TPU:1, one launch (start us, length us, event | category | flops | bytes accessed | tf_op | source)
XLA Modules:
  0.0 95.3 jit_solution(14323689768177724147)
XLA Ops:
  0.0 0.0 copy-start.1
  0.0 0.8 and_convert_fusion
  0.9 0.1 copy.17
  0.9 1.0 %convert_element_type.4 = bf16[16,4,1024]{2,1,0:T(4,128)(2,1)S(1)} convert(f32[16,4,1024]{2,1,0:T(4,128)} %param.13) | non-fusion elementwise | flops 65536 | bytes 393216 | tf_op jit(solution)/shard_map/convert_element_type | solution.py:277
  2.0 0.1 reshape.19
  2.0 1.0 %reshape.18 = bf16[16,2,16,128]{3,2,1,0:T(8,128)(2,1)S(1)} reshape(bf16[16,4,1024]{2,1,0:T(4,128)(2,1)} %param.14) | data formatting | bytes 262144 | tf_op jit(solution)/shard_map/reshape | solution.py:276
  3.0 0.0 copy-start.3
  3.0 0.0 copy-start.4
  3.0 0.0 copy-start.7
  3.1 19.2 %all_to_all.20.ex_ref = bf16[2,33,16,128]{3,2,1,0:T(8,128)(2,1)S(1)} all-to-all(bf16[2,33,16,128]{3,2,1,0:T(8,128)(2,1)S(1)} %maximum_bitcast_fusion), channel_id=1, replica_groups=mesh['zh'=2,'j'=32,'chan'=8] {'zh'}, dimensions={0} | all-to-all | bytes 540672 | tf_op jit(solution)/shard_map/all_to_all | solution.py:281
  22.2 0.0 copy-start.2
  22.2 0.0 copy-start.5
  22.2 0.0 copy-start.6
  22.3 6.7 %collective-permute-start.1 = (bf16[2,4,16,128]{3,2,1,0:T(8,128)(2,1)S(1)}, bf16[2,4,16,128]{3,2,1,0:T(8,128)(2,1)S(1)}, u32[]{:S(2)}, u32[]{:S(2)}) collective-permute-start(bf16[2,4,16,128]{3,2,1,0:T(8,128)(2,1)S(1)} %pad_maximum_fusion.1), channel_id=1, source_target_pairs={{8,0},{16,8},{24,16},{32,24},{40,32},{48,40},{56,48},{64,56},{72,6... | collective-permute-start | bytes 98312 | tf_op jit(solution)/shard_map/ppermute | solution.py:285
  28.9 3.0 %collective-permute-start = (bf16[2,4,16,128]{3,2,1,0:T(8,128)(2,1)S(1)}, bf16[2,4,16,128]{3,2,1,0:T(8,128)(2,1)S(1)}, u32[]{:S(2)}, u32[]{:S(2)}) collective-permute-start(bf16[2,4,16,128]{3,2,1,0:T(8,128)(2,1)S(1)} %pad_maximum_fusion), channel_id=1, source_target_pairs={{0,8},{8,16},{16,24},{24,32},{32,40},{40,48},{48,56},{56,64},{64,7... | collective-permute-start | bytes 98312 | tf_op jit(solution)/shard_map/ppermute | solution.py:284
  32.0 0.0 collective-permute-done.1.high_ref
  32.0 1.0 %collective-permute-done.low_ref = bf16[2,4,16,128]{3,2,1,0:T(8,128)(2,1)S(1)} collective-permute-done((bf16[2,4,16,128]{3,2,1,0:T(8,128)(2,1)S(1)}, bf16[2,4,16,128]{3,2,1,0:T(8,128)(2,1)S(1)}, u32[]{:S(2)}, u32[]{:S(2)}) %collective-permute-start) | collective-permute-done | bytes 32800 | tf_op jit(solution)/shard_map/ppermute | solution.py:284
  33.0 0.0 copy-done.1
  33.0 5.8 %shard_map.118 = bf16[32,16,128]{2,1,0:T(8,128)(2,1)S(1)} custom-call(bf16[2,33,16,128]{3,2,1,0:T(8,128)(2,1)S(1)} %all_to_all.20.ex_ref, bf16[2,4,16,128]{3,2,1,0:T(8,128)(2,1)S(1)} %collective-permute-done.low_ref, bf16[2,4,16,128]{3,2,1,0:T(8,128)(2,1)S(1)} %collective-permute-done.1.high_ref, bf16[1024,1024]{1,0:T(8,128)(2,1)S(1)} %copy-done.1), custom_call_target="tpu_custom_call" | custom-call | tf_op jit(solution)/shard_map/pallas_call | solution.py:286
  38.7 0.0 copy-start
  38.7 18.7 %all_to_all.21 = bf16[32,16,128]{2,1,0:T(8,128)(2,1)S(1)} all-to-all(bf16[32,16,128]{2,1,0:T(8,128)(2,1)S(1)} %shard_map.118), channel_id=1, replica_groups=mesh['zh'=2,'j'=32,'chan'=8] {'j'}, dimensions={0} | all-to-all | bytes 262144 | tf_op jit(solution)/shard_map/all_to_all | solution.py:302
  57.4 0.0 copy-done.3
  57.5 0.0 copy-done.4
  57.5 0.0 copy-done.7
  57.5 1.3 %shard_map.119 = (f32[256,256]{1,0:T(8,128)S(1)}, f32[16,8,128]{2,1,0:T(8,128)}) custom-call(bf16[512,128]{1,0:T(8,128)(2,1)S(1)} %bitcast.6, bf16[256,256]{1,0:T(8,128)(2,1)S(1)} %copy-done.7, f32[256,256]{1,0:T(8,128)S(1)} %copy-done.3, bf16[512,256]{1,0:T(8,128)(2,1)S(1)} %copy-done.4), custom_call_target="tpu_custom_call" | custom-call | tf_op jit(solution)/shard_map/pallas_call | solution.py:304
  58.8 6.9 %all-to-all-start.2 = ((f32[16,8,128]{2,1,0:T(8,128)}), f32[16,8,128]{2,1,0:T(8,128)S(1)}, u32[]{:S(2)}, u32[]{:S(2)}) async-start(f32[16,8,128]{2,1,0:T(8,128)} %get-tuple-element.8), calls=%async_computation.2 | async-start | bytes 131072 | tf_op jit(solution)/shard_map/all_to_all | solution.py:310
  66.3 10.6 %all-to-all-done.2.peak_ref = f32[16,8,128]{2,1,0:T(8,128)S(1)} async-done(((f32[16,8,128]{2,1,0:T(8,128)}), f32[16,8,128]{2,1,0:T(8,128)S(1)}, u32[]{:S(2)}, u32[]{:S(2)}) %all-to-all-start.2) | async-done | bytes 65568 | tf_op jit(solution)/shard_map/all_to_all | solution.py:310
  77.0 0.0 copy-done.2
  77.0 0.0 copy-done.5
  77.0 0.0 copy-done.6
  77.0 0.5 shard_map.120
  77.5 16.5 %all_to_all.22 = bf16[64,8,128]{2,1,0:T(8,128)(2,1)S(1)} all-to-all(bf16[64,8,128]{2,1,0:T(8,128)(2,1)S(1)} %bitcast.7), channel_id=1, replica_groups=mesh['zh'=2,'j'=32,'chan'=8] {'zh','j'}, dimensions={0} | all-to-all | bytes 262144 | tf_op jit(solution)/shard_map/all_to_all | solution.py:317
  94.0 0.0 copy-done
  94.1 1.3 %shard_map.121 = f32[16,4,1024]{2,1,0:T(4,128)} custom-call(bf16[512,128]{1,0:T(8,128)(2,1)S(1)} %bitcast.5, bf16[1024,1024]{1,0:T(8,128)(2,1)S(1)} %copy-done), custom_call_target="tpu_custom_call" | custom-call | tf_op jit(solution)/shard_map/pallas_call | solution.py:318
  (8 shorter events, 0.1 us)
Async XLA Ops:
  0.0 33.0 %copy-start.1 = (bf16[1024,1024]{1,0:T(8,128)(2,1)S(1)}, bf16[1024,1024]{1,0:T(8,128)(2,1)}, u32[]{:S(2)}) copy-start(bf16[1024,1024]{1,0:T(8,128)(2,1)} %constant.23.clone.table_hbm) | copy-start | bytes 6291460
  3.0 54.5 %copy-start.3 = (f32[256,256]{1,0:T(8,128)S(1)}, f32[256,256]{1,0:T(8,128)}, u32[]{:S(2)}) copy-start(f32[256,256]{1,0:T(8,128)} %constant.25.clone.turn_ref) | copy-start | bytes 786436
  3.0 54.4 %copy-start.4 = (bf16[512,256]{1,0:T(8,128)(2,1)S(1)}, bf16[512,256]{1,0:T(8,128)(2,1)}, u32[]{:S(2)}) copy-start(bf16[512,256]{1,0:T(8,128)(2,1)} %constant.26.clone.shots_ref) | copy-start | bytes 786436
  3.0 54.4 %copy-start.7 = (bf16[256,256]{1,0:T(8,128)(2,1)S(1)}, bf16[256,256]{1,0:T(8,128)(2,1)}, u32[]{:S(2)}) copy-start(bf16[256,256]{1,0:T(8,128)(2,1)} %constant.24.clone.merge_ref) | copy-start | bytes 393220
  22.2 54.7 %copy-start.2 = (bf16[512,512]{1,0:T(8,128)(2,1)S(1)}, bf16[512,512]{1,0:T(8,128)(2,1)}, u32[]{:S(2)}) copy-start(bf16[512,512]{1,0:T(8,128)(2,1)} %constant.29.clone.split_ref) | copy-start | bytes 1572868
  22.2 54.7 %copy-start.5 = (bf16[512,256]{1,0:T(8,128)(2,1)S(1)}, bf16[512,256]{1,0:T(8,128)(2,1)}, u32[]{:S(2)}) copy-start(bf16[512,256]{1,0:T(8,128)(2,1)} %constant.27.clone.shots_ref) | copy-start | bytes 786436
  22.2 54.7 %copy-start.6 = (f32[256,256]{1,0:T(8,128)S(1)}, f32[256,256]{1,0:T(8,128)}, u32[]{:S(2)}) copy-start(f32[256,256]{1,0:T(8,128)} %constant.28.clone.turn_ref) | copy-start | bytes 786436
  22.3 9.7 %collective-permute-start.1 = (bf16[2,4,16,128]{3,2,1,0:T(8,128)(2,1)S(1)}, bf16[2,4,16,128]{3,2,1,0:T(8,128)(2,1)S(1)}, u32[]{:S(2)}, u32[]{:S(2)}) collective-permute-start(bf16[2,4,16,128]{3,2,1,0:T(8,128)(2,1)S(1)} %pad_maximum_fusion.1), channel_id=1, source_target_pairs={{8,0},{16,8},{24,16},{32,24},{40,32},{48,40},{56,48},{64,56},{72,6... | collective-permute-start | bytes 98312 | tf_op jit(solution)/shard_map/ppermute | solution.py:285
  28.9 4.0 %collective-permute-start = (bf16[2,4,16,128]{3,2,1,0:T(8,128)(2,1)S(1)}, bf16[2,4,16,128]{3,2,1,0:T(8,128)(2,1)S(1)}, u32[]{:S(2)}, u32[]{:S(2)}) collective-permute-start(bf16[2,4,16,128]{3,2,1,0:T(8,128)(2,1)S(1)} %pad_maximum_fusion), channel_id=1, source_target_pairs={{0,8},{8,16},{16,24},{24,32},{32,40},{40,48},{48,56},{56,64},{64,7... | collective-permute-start | bytes 98312 | tf_op jit(solution)/shard_map/ppermute | solution.py:284
  38.7 55.3 %copy-start = (bf16[1024,1024]{1,0:T(8,128)(2,1)S(1)}, bf16[1024,1024]{1,0:T(8,128)(2,1)}, u32[]{:S(2)}) copy-start(bf16[1024,1024]{1,0:T(8,128)(2,1)} %constant.30.clone.table_ref) | copy-start | bytes 6291460
  58.8 18.2 %all-to-all-start.2 = ((f32[16,8,128]{2,1,0:T(8,128)}), f32[16,8,128]{2,1,0:T(8,128)S(1)}, u32[]{:S(2)}, u32[]{:S(2)}) async-start(f32[16,8,128]{2,1,0:T(8,128)} %get-tuple-element.8), calls=%async_computation.2 | async-start | bytes 131072 | tf_op jit(solution)/shard_map/all_to_all | solution.py:310

commit v2 on v0

v2 whole, which is shorter than its diff:
```python
import jax
import jax.numpy as jnp
import numpy as np
from jax import lax
from jax.experimental import pallas as pl
from jax.experimental.pallas import tpu as pltpu
from jax.sharding import PartitionSpec as P

SHOTS, SAMPLES, FREQS = 1024, 1024, 512
DEVS, BLOCK, CHANS = 64, 16, 4
STEP = 24
INTERPRET = False


def time_table():
    t = np.arange(SAMPLES)[None, :]
    k = np.arange(FREQS)[:, None]
    phase = 2 * np.pi * ((t * k) % SAMPLES) / SAMPLES
    return (np.concatenate([np.cos(phase), -np.sin(phase)], 0) / 32).astype(jnp.bfloat16)


def time_back_table():
    t = np.arange(SAMPLES)[None, :]
    k = np.arange(FREQS)[:, None]
    phase = 2 * np.pi * ((t * k) % SAMPLES) / SAMPLES
    weight = np.where(k == 0, 1.0, 2.0) / 32
    return np.concatenate([weight * np.cos(phase), -weight * np.sin(phase)], 0).astype(jnp.bfloat16)


def place_table():
    phase = 2 * np.pi * (np.arange(64)[:, None] * np.arange(64)[None, :] % 64) / 64
    return np.concatenate([np.cos(phase), np.sin(phase)], 0).astype(jnp.bfloat16)


def twiddles():
    phase = 2 * np.pi * np.arange(64)[:, None] * np.arange(BLOCK)[None, :] / SHOTS
    cos, sin = np.tile(np.cos(phase), (1, 8)), np.tile(np.sin(phase), (1, 8))
    sin[:, 64:] *= -1
    return np.concatenate([cos, sin], 1).astype(np.float32)


def block_table(sign):
    out = np.zeros((2, CHANS, 16, 2, CHANS, 16), np.float64)
    phase = 2 * np.pi * (np.arange(16)[:, None] * np.arange(16)[None, :] % 16) / 16
    for c in range(CHANS):
        out[0, c, :, 0, c, :] = np.cos(phase)
        out[1, c, :, 1, c, :] = np.cos(phase)
        out[0, c, :, 1, c, :] = sign * np.sin(phase)
        out[1, c, :, 0, c, :] = -sign * np.sin(phase)
    return (out.reshape(128, 128) / 32).astype(jnp.bfloat16)


def lane_ids(*shape):
    return lax.broadcasted_iota(jnp.int32, (*shape, 128), len(shape))


def swapped(value):
    return pltpu.roll(value, 64, value.ndim - 1)


def blend_kernel(lag_ref, dat_ref, est_ref, table_hbm, out_ref, tmp, est, res, upd, acc, table, sem):
    copy = pltpu.make_async_copy(table_hbm, table, sem)
    copy.start()
    place = lax.axis_index("shot")
    est[...] = jnp.zeros_like(est)
    res[...] = jnp.zeros_like(res)
    upd[1024:, :] = jnp.zeros((1024, 128), jnp.float32)
    tmp[...] = est_ref[...].astype(jnp.float32)

    def base(row, c):
        return (row * CHANS + c) * STEP + 16

    for c in range(CHANS):
        for u in range(8):
            columns = slice(128 * u, 128 * u + 128)
            old = tmp[:, c, columns]
            est[pl.ds(base(2, c) + u, BLOCK, stride=CHANS * STEP), :] = old
            res[pl.ds(base(3, c) + u, BLOCK, stride=CHANS * STEP), :] = dat_ref[:, c, columns] - old

    lanes = lane_ids(8)

    def companions(ref, row_of, side, n, kinds):
        shot = (512 * side + BLOCK * place + n + SHOTS) & (SHOTS - 1)
        fleet = ((shot + 1) >> 9) & 1
        own = (shot & 15) * 6 + 3 * fleet
        other = (shot & 15) * 6 + 3 - 3 * fleet
        slots = ((own, 0, -1), (own + 2, 0, 1), (other, 1, -1), (other + 1, 1, 0), (other + 2, 1, 1))
        total = [None] * CHANS
        for at, flip, step in slots:
            if flip not in kinds:
                continue
            lag = lag_ref[shot >> 4, at]
            turn = lag & 127
            keep = lanes < 128 - turn
            first = base(row_of(side ^ flip, n + step), 0) - (lag >> 7)
            for c in range(CHANS):
                here = ref[pl.ds(first + c * STEP, 8), :]
                before = ref[pl.ds(first + c * STEP - 1, 8), :]
                moved = pltpu.roll(jnp.where(keep, here, before), turn, 1)
                total[c] = moved if total[c] is None else total[c] + moved
        return total

    def est_row(side, n):
        return n + 2

    def res_row(side, n):
        return side * 22 + n + 3

    @pl.loop(0, BLOCK + 2)
    def _(step):
        n = step - 1
        near = companions(est, est_row, 0, n, (0,))
        far = companions(est, est_row, 1, n, (1,))
        for c in range(CHANS):
            rows = pl.ds(base(res_row(0, n), c), 8)
            res[rows, :] = res[rows, :] - near[c]
            res[pl.ds(base(res_row(1, n), c), 8), :] = -far[c]

    @pl.loop(0, BLOCK + 4)
    def _(step):
        n = step - 2
        for side in range(2):
            total = companions(res, res_row, side, n, (0, 1))
            low = 128 + (14 if side == 0 else 12) + n + 2
            high = 128 + (0 if side == 0 else 2) + n - 16
            at = jnp.where(n < 0, low, jnp.where(n > 15, high, side * 64 + n))
            for c in range(CHANS):
                value = 0.25 * (total[c] + res[pl.ds(base(res_row(side, n), c), 8), :])
                if side == 0:
                    value = value + est[pl.ds(base(n + 2, c), 8), :]
                upd[pl.ds((at + c * BLOCK) * 8, 8), :] = value

    rows = jnp.concatenate([upd[pl.ds(u, 256, stride=8), :] for u in range(8)], 1).astype(jnp.bfloat16)
    copy.wait()
    rims = None
    for ri in range(2):
        product = lax.dot_general(
            table[512 * ri : 512 * ri + 512, :],
            rows,
            (((1,), (1,)), ((), ())),
            preferred_element_type=jnp.float32,
        )
        acc[:, 8 * ri : 8 * ri + 8, :] = product[:, :128].reshape(DEVS, 8, 128)
        rims = product[:, 128:] if rims is None else rims + swapped(product[:, 128:])
    acc[:, 16:24, :] = rims.reshape(DEVS, 8, 128)
    out_ref[...] = acc[...].reshape(DEVS * 24, 128).astype(jnp.bfloat16)


def forward_kernel(x_ref, place_ref, turn_ref, block_ref, spec_ref, peak_ref, tmp):
    x = x_ref[...].astype(jnp.float32).reshape(DEVS, 24, 128)
    real, imag, rims = x[:, :8], x[:, 8:16], x[:, 16:]

    def ahead(value, count):
        return jnp.concatenate([value[count:], value[:count]], 0)

    def lane_roll(value, shift):
        return pltpu.roll(value.reshape(512, 128), shift, 1).reshape(DEVS, 8, 128)

    lanes = lane_ids(DEVS, 8)
    within = lanes & 15
    total = jnp.where(
        lanes < 64,
        real + lane_roll(ahead(real, 32), 64),
        lane_roll(imag, 64) + ahead(imag, 32),
    )
    far = ahead(rims, 32)
    rims = rims + jnp.where(within < 8, lane_roll(far, 126), lane_roll(far, 2))
    total = total + jnp.where(within < 2, ahead(rims, 63), jnp.where(within >= 14, ahead(rims, 1), 0.0))
    tmp[...] = total.reshape(512, 128)
    rhs = jnp.concatenate([tmp[pl.ds(kk, 64, stride=8), :] for kk in range(8)], 1).astype(jnp.bfloat16)
    product = jnp.dot(place_ref[...], rhs, preferred_element_type=jnp.float32)
    cos, sin = turn_ref[:, :128], turn_ref[:, 128:]
    half = lane_ids(64) < 64
    turned = []
    for kk in range(8):
        columns = slice(128 * kk, 128 * kk + 128)
        other = swapped(product[64:, columns])
        value = product[:64, columns] + jnp.where(half, other, -other)
        turned.append((value * cos + swapped(value) * sin).astype(jnp.bfloat16))
    spec = jnp.dot(jnp.concatenate(turned, 0), block_ref[...], preferred_element_type=jnp.float32)
    spec_ref[...] = spec
    square = spec * spec
    square = square + swapped(square)
    peak = jnp.concatenate(
        [jnp.max(square[64 * kk : 64 * kk + 64], axis=0, keepdims=True) for kk in range(8)], 0
    )
    for shift in (1, 2, 4, 8, 16, 32):
        peak = jnp.maximum(peak, pltpu.roll(peak, shift, 1))
    peak_ref[...] = jnp.broadcast_to(peak[None], peak_ref.shape)


def backward_kernel(level_ref, spec_ref, peak_ref, place_ref, turn_ref, block_ref, out_ref, tmp):
    peak = jnp.sqrt(jnp.max(peak_ref[...], axis=0))
    limit = level_ref[0].astype(jnp.float32) * (1 / 64) * (peak + 1e-6)
    shrunk = []
    for kk in range(8):
        value = spec_ref[64 * kk : 64 * kk + 64, :]
        square = value * value
        size = jnp.sqrt(square + swapped(square))
        bound = limit[kk : kk + 1]
        factor = jnp.maximum(size - bound, 0.0) / jnp.maximum(size, bound)
        shrunk.append((value * factor).astype(jnp.bfloat16))
    product = jnp.dot(jnp.concatenate(shrunk, 0), block_ref[...], preferred_element_type=jnp.float32)
    cos, sin = turn_ref[:, :128], turn_ref[:, 128:]
    turned = []
    for kk in range(8):
        value = product[64 * kk : 64 * kk + 64]
        turned.append((value * cos - swapped(value) * sin).astype(jnp.bfloat16))
    product = jnp.dot(place_ref[...], jnp.concatenate(turned, 1), preferred_element_type=jnp.float32)
    half = lane_ids(64) < 64
    for kk in range(8):
        columns = slice(128 * kk, 128 * kk + 128)
        other = swapped(product[64:, columns])
        tmp[pl.ds(kk, 64, stride=8), :] = product[:64, columns] - jnp.where(half, other, -other)
    out_ref[...] = tmp[...].astype(jnp.bfloat16)


def time_back_kernel(x_ref, table_ref, out_ref):
    turned = x_ref[...].astype(jnp.float32).T.astype(jnp.bfloat16)
    left = jnp.concatenate([turned[:64], turned[64:]], 1)
    for n in range(4):
        columns = slice(256 * n, 256 * n + 256)
        product = jnp.dot(left, table_ref[:, columns], preferred_element_type=jnp.float32)
        for c in range(CHANS):
            out_ref[:, c, columns] = product[BLOCK * c : BLOCK * c + BLOCK]


def vmem(count):
    return [pl.BlockSpec(memory_space=pltpu.VMEM)] * count


def smem():
    return pl.BlockSpec(memory_space=pltpu.SMEM)


def call(kernel, outs, in_specs, scratch=()):
    return pl.pallas_call(
        kernel,
        out_shape=outs,
        in_specs=in_specs,
        out_specs=vmem(len(outs)) if isinstance(outs, list) else vmem(1)[0],
        scratch_shapes=list(scratch),
        compiler_params=pltpu.CompilerParams(vmem_limit_bytes=32 * 1024 * 1024),
        interpret=INTERPRET,
    )


def local(blended, estimate, neighbour_sources, partner_lags, threshold_level):
    lags = jnp.pad(partner_lags.reshape(-1), (0, 32))
    lags = lax.all_to_all(jnp.broadcast_to(lags, (DEVS, 128)), "shot", 0, 0, tiled=True)
    send = call(
        blend_kernel,
        jax.ShapeDtypeStruct((DEVS * 24, 128), jnp.bfloat16),
        [smem()] + vmem(2) + [pl.BlockSpec(memory_space=pl.ANY)],
        [
            pltpu.VMEM((BLOCK, CHANS, SAMPLES), jnp.float32),
            pltpu.VMEM((20 * CHANS * STEP + 16, 128), jnp.float32),
            pltpu.VMEM((44 * CHANS * STEP + 16, 128), jnp.float32),
            pltpu.VMEM((2048, 128), jnp.float32),
            pltpu.VMEM((DEVS, 24, 128), jnp.float32),
            pltpu.VMEM((SAMPLES, SAMPLES), jnp.bfloat16),
            pltpu.SemaphoreType.DMA,
        ],
    )(lags, blended, estimate, time_table())
    columns = lax.all_to_all(send.reshape(DEVS, 24, 128), "shot", 0, 0, tiled=True).reshape(DEVS * 24, 128)
    others = lax.axis_size("chan")
    spec, peak = call(
        forward_kernel,
        [jax.ShapeDtypeStruct((512, 128), jnp.float32), jax.ShapeDtypeStruct((others, 8, 128), jnp.float32)],
        vmem(4),
        [pltpu.VMEM((512, 128), jnp.float32)],
    )(columns, place_table(), twiddles(), block_table(-1))
    peaks = lax.all_to_all(peak, "chan", 0, 0, tiled=True)
    back = call(
        backward_kernel,
        jax.ShapeDtypeStruct((512, 128), jnp.bfloat16),
        [smem()] + vmem(5),
        [pltpu.VMEM((512, 128), jnp.float32)],
    )(threshold_level, spec, peaks, place_table(), twiddles(), block_table(1))
    arrived = lax.all_to_all(back.reshape(DEVS, 8, 128), "shot", 0, 0, tiled=True).reshape(512, 128)
    return call(
        time_back_kernel,
        jax.ShapeDtypeStruct((BLOCK, CHANS, SAMPLES), jnp.float32),
        vmem(2),
    )(arrived, time_back_table())


def solution(mesh):
    shots = P("shot", "chan", None)
    return jax.shard_map(
        local,
        mesh=mesh,
        in_specs=(shots, shots, P("shot", None), P("shot", None), P()),
        out_specs=shots,
        check_vma=False,
    )
```

time: 351 us -> 90.6 us (0.26)
  blocking collectives: 298 us -> 61 us
  starting transfers between devices: 20.5 us -> 6.81 us
  local copies, waits for them, and re-layouts: 9.54 us -> 4.37 us
  waiting for transfers between devices: 10.6 us -> 6.25 us
    unnamed x1 -> x0, blocking collectives: 243 us -> none
    ppermute x2 -> x0, starting transfers between devices: 9.43 us -> none  [the longest x1 6.42 us: local(): lax.ppermute(down, 'j', [((i + 1) % PLACES, i) for i in range(PLACES)])]
    all_to_all x3, blocking collectives: 54.3 us -> 61 us  [the longest x1 24 us: local(): lax.all_to_all(jnp.broadcast_to(lags, (DEVS, 128)), 'shot', 0, 0, tiled=T...]
    all_to_all x1, waiting for transfers between devices: 10.6 us -> 6.25 us  [local(): peaks = lax.all_to_all(peak, 'chan', 0, 0, tiled=True)]
    all_to_all x1, starting transfers between devices: 11.1 us -> 6.81 us  [local(): peaks = lax.all_to_all(peak, 'chan', 0, 0, tiled=True)]
    unnamed x26 -> x17, local copies, waits for them, and re-layouts: 8.41 us -> 4.26 us
  transfers between devices with their start and end apart: 3 -> 1, of which waited for: 1 -> 1; matrix products, arithmetic and copies ran while one was open for 1% -> 0% of each run, Pallas kernels for 0% -> 0%
where the time goes in v2:
time: 90.6 us; the launch traced here: 90.2 us
  blocking collectives  61 us (67%)
  Pallas kernels  11 us (12%)
  starting transfers between devices  6.81 us (8%)
  waiting for transfers between devices  6.25 us (7%)
  local copies, waits for them, and re-layouts  4.37 us (5%)
    all_to_all x1, blocking collectives, local(): lax.all_to_all(jnp.broadcast_to(lags, (DEVS, 128)), 'shot', 0, 0, tiled=T...  24 us
    all_to_all x1, blocking collectives, local(): lax.all_to_all(send.reshape(DEVS, 24, 128), 'shot', 0, 0, tiled=True)  19.1 us
    all_to_all x1, blocking collectives, local(): lax.all_to_all(back.reshape(DEVS, 8, 128), 'shot', 0, 0, tiled=True)  17.9 us
    pallas_call x1, Pallas kernels, local(): call(blend_kernel, jax.ShapeDtypeStruct((DEVS * 24, 128), jnp.bfloat16),...  7.25 us
    all_to_all x1, starting transfers between devices, local(): peaks = lax.all_to_all(peak, 'chan', 0, 0, tiled=True)  6.81 us
    all_to_all x1, waiting for transfers between devices, local(): peaks = lax.all_to_all(peak, 'chan', 0, 0, tiled=True)  6.25 us
    unnamed x17, local copies, waits for them, and re-layouts  4.26 us
    pallas_call x1, Pallas kernels, local(): call(forward_kernel, [jax.ShapeDtypeStruct((512, 128), jnp.float32), jax....  1.87 us
  transfers between devices with their start and end apart: 1, of which 1 were waited for; matrix products, arithmetic and copies ran while one was open for 0% of the time, Pallas kernels for 0%

profile of v2, /device:TPU:1, one launch (start us, length us, event | category | flops | bytes accessed | tf_op | source)
XLA Modules:
  0.0 90.2 jit_solution(15958291524376416692)
XLA Ops:
  0.0 0.0 copy-start.5
  0.0 0.0 copy-start.3
  0.0 0.0 copy-start.7
  0.0 0.8 copy.15
  0.8 0.1 reshape.19
  0.9 24.0 %all_to_all.23 = s32[64,1,128]{2,1,0:T(1,128)S(1)} all-to-all(s32[64,1,128]{2,1,0:T(1,128)S(1)} %broadcast_in_dim.3), channel_id=1, replica_groups=mesh['shot'=64,'chan'=8] {'shot'}, dimensions={0} | all-to-all | bytes 65536 | tf_op jit(solution)/shard_map/all_to_all | solution.py:250
  24.9 0.0 copy-start.1
  25.0 1.6 %copy-done.1 = bf16[1024,1024]{1,0:T(8,128)(2,1)S(1)} copy-done((bf16[1024,1024]{1,0:T(8,128)(2,1)S(1)}, bf16[1024,1024]{1,0:T(8,128)(2,1)}, u32[]{:S(2)}) %copy-start.1) | copy-done | bytes 2097176
  26.5 0.0 copy-start.2
  26.5 0.9 %copy-done.2 = f32[16,4,1024]{2,1,0:T(4,128)S(1)} copy-done((f32[16,4,1024]{2,1,0:T(4,128)S(1)}, f32[16,4,1024]{2,1,0:T(4,128)}, u32[]{:S(2)}) %copy-start.2) | copy-done | bytes 262168
  27.5 0.0 copy-start.4
  27.5 0.9 %copy-done.4 = bf16[16,4,1024]{2,1,0:T(4,128)(2,1)S(1)} copy-done((bf16[16,4,1024]{2,1,0:T(4,128)(2,1)S(1)}, bf16[16,4,1024]{2,1,0:T(4,128)(2,1)}, u32[]{:S(2)}) %copy-start.4) | copy-done | bytes 131096
  28.4 0.0 copy-start.6
  28.4 0.0 copy-start
  28.4 7.2 %shard_map.118 = bf16[1536,128]{1,0:T(8,128)(2,1)S(1)} custom-call(s32[64,128]{1,0:T(8,128)S(1)} %bitcast.9, f32[16,4,1024]{2,1,0:T(4,128)S(1)} %copy-done.2, bf16[16,4,1024]{2,1,0:T(4,128)(2,1)S(1)} %copy-done.4, bf16[1024,1024]{1,0:T(8,128)(2,1)S(1)} %copy-done.1), custom_call_target="tpu_custom_call" | custom-call | tf_op jit(solution)/shard_map/pallas_call | solution.py:251
  35.7 19.1 %all_to_all.24 = bf16[64,24,128]{2,1,0:T(8,128)(2,1)S(1)} all-to-all(bf16[64,24,128]{2,1,0:T(8,128)(2,1)S(1)} %bitcast.6), channel_id=1, replica_groups=mesh['shot'=64,'chan'=8] {'shot'}, dimensions={0} | all-to-all | bytes 786432 | tf_op jit(solution)/shard_map/all_to_all | solution.py:265
  54.8 0.0 copy-done.5
  54.8 0.0 copy-done.3
  54.8 0.0 copy-done.7
  54.8 1.9 %shard_map.119 = (f32[512,128]{1,0:T(8,128)S(1)}, f32[8,8,128]{2,1,0:T(8,128)}) custom-call(bf16[1536,128]{1,0:T(8,128)(2,1)S(1)} %bitcast.5, bf16[128,64]{1,0:T(8,128)(2,1)S(1)} %copy-done.5, f32[64,256]{1,0:T(8,128)S(1)} %copy-done.3, bf16[128,128]{1,0:T(8,128)(2,1)S(1)} %copy-done.7), custom_call_target="tpu_custom_call" | custom-call | tf_op jit(solution)/shard_map/pallas_call | solution.py:267
  56.6 6.8 %all-to-all-start.2 = ((f32[8,8,128]{2,1,0:T(8,128)}), f32[8,8,128]{2,1,0:T(8,128)S(1)}, u32[]{:S(2)}, u32[]{:S(2)}) async-start(f32[8,8,128]{2,1,0:T(8,128)} %get-tuple-element.8), calls=%async_computation.2 | async-start | bytes 65536 | tf_op jit(solution)/shard_map/all_to_all | solution.py:273
  64.1 6.3 %all-to-all-done.2.peak_ref = f32[8,8,128]{2,1,0:T(8,128)S(1)} async-done(((f32[8,8,128]{2,1,0:T(8,128)}), f32[8,8,128]{2,1,0:T(8,128)S(1)}, u32[]{:S(2)}, u32[]{:S(2)}) %all-to-all-start.2) | async-done | bytes 32800 | tf_op jit(solution)/shard_map/all_to_all | solution.py:273
  70.4 0.0 copy-done.6
  70.4 0.6 shard_map.120
  71.0 17.9 %all_to_all.25 = bf16[64,8,128]{2,1,0:T(8,128)(2,1)S(1)} all-to-all(bf16[64,8,128]{2,1,0:T(8,128)(2,1)S(1)} %bitcast.7), channel_id=1, replica_groups=mesh['shot'=64,'chan'=8] {'shot'}, dimensions={0} | all-to-all | bytes 262144 | tf_op jit(solution)/shard_map/all_to_all | solution.py:280
  88.9 0.0 copy-done
  88.9 1.3 %shard_map.121 = f32[16,4,1024]{2,1,0:T(4,128)} custom-call(bf16[512,128]{1,0:T(8,128)(2,1)S(1)} %bitcast.8, bf16[1024,1024]{1,0:T(8,128)(2,1)S(1)} %copy-done), custom_call_target="tpu_custom_call" | custom-call | tf_op jit(solution)/shard_map/pallas_call | solution.py:281
  (2 shorter events, 0.0 us)
Async XLA Ops:
  0.0 54.8 %copy-start.5 = (bf16[128,64]{1,0:T(8,128)(2,1)S(1)}, bf16[128,64]{1,0:T(8,128)(2,1)}, u32[]{:S(2)}) copy-start(bf16[128,64]{1,0:T(8,128)(2,1)} %constant.15.clone.place_ref) | copy-start | bytes 49156
  0.0 54.8 %copy-start.3 = (f32[64,256]{1,0:T(8,128)S(1)}, f32[64,256]{1,0:T(8,128)}, u32[]{:S(2)}) copy-start(f32[64,256]{1,0:T(8,128)} %constant.16.clone.turn_ref) | copy-start | bytes 196612
  0.0 54.8 %copy-start.7 = (bf16[128,128]{1,0:T(8,128)(2,1)S(1)}, bf16[128,128]{1,0:T(8,128)(2,1)}, u32[]{:S(2)}) copy-start(bf16[128,128]{1,0:T(8,128)(2,1)} %constant.17.clone.block_ref) | copy-start | bytes 98308
  24.9 1.6 %copy-start.1 = (bf16[1024,1024]{1,0:T(8,128)(2,1)S(1)}, bf16[1024,1024]{1,0:T(8,128)(2,1)}, u32[]{:S(2)}) copy-start(bf16[1024,1024]{1,0:T(8,128)(2,1)} %constant.14.clone.table_hbm) | copy-start | bytes 6291460
  26.5 0.9 %copy-start.2 = (f32[16,4,1024]{2,1,0:T(4,128)S(1)}, f32[16,4,1024]{2,1,0:T(4,128)}, u32[]{:S(2)}) copy-start(f32[16,4,1024]{2,1,0:T(4,128)} %dat_ref.1) | copy-start | bytes 786436
  27.5 0.9 %copy-start.4 = (bf16[16,4,1024]{2,1,0:T(4,128)(2,1)S(1)}, bf16[16,4,1024]{2,1,0:T(4,128)(2,1)}, u32[]{:S(2)}) copy-start(bf16[16,4,1024]{2,1,0:T(4,128)(2,1)} %est_ref.1) | copy-start | bytes 393220
  28.4 42.0 %copy-start.6 = (bf16[128,128]{1,0:T(8,128)(2,1)S(1)}, bf16[128,128]{1,0:T(8,128)(2,1)}, u32[]{:S(2)}) copy-start(bf16[128,128]{1,0:T(8,128)(2,1)} %constant.18.clone.block_ref) | copy-start | bytes 98308
  28.4 60.5 %copy-start = (bf16[1024,1024]{1,0:T(8,128)(2,1)S(1)}, bf16[1024,1024]{1,0:T(8,128)(2,1)}, u32[]{:S(2)}) copy-start(bf16[1024,1024]{1,0:T(8,128)(2,1)} %constant.19.clone.table_ref) | copy-start | bytes 6291460
  56.6 13.7 %all-to-all-start.2 = ((f32[8,8,128]{2,1,0:T(8,128)}), f32[8,8,128]{2,1,0:T(8,128)S(1)}, u32[]{:S(2)}, u32[]{:S(2)}) async-start(f32[8,8,128]{2,1,0:T(8,128)} %get-tuple-element.8), calls=%async_computation.2 | async-start | bytes 65536 | tf_op jit(solution)/shard_map/all_to_all | solution.py:273

commit v3 on v2

--- a/solution.py
+++ b/solution.py
@@ -58,77 +58,89 @@
     return pltpu.roll(value, 64, value.ndim - 1)
 
 
-def blend_kernel(lag_ref, dat_ref, est_ref, table_hbm, out_ref, tmp, est, res, upd, acc, table, sem):
-    copy = pltpu.make_async_copy(table_hbm, table, sem)
-    copy.start()
+def base(row, c):
+    return (row * CHANS + c) * STEP + 16
+
+
+def res_row(side, n):
+    return side * 22 + n + 3
+
+
+def place_of(side, n):
+    low = 128 + (14 if side == 0 else 12) + n + 2
+    high = 128 + (0 if side == 0 else 2) + n - 16
+    return jnp.where(n < 0, low, jnp.where(n > 15, high, side * 64 + n))
+
+
+def add_shifted(total, ref, first, lag, lanes):
+    turn = lag & 127
+    keep = lanes < 128 - turn
+    first = first - (lag >> 7)
+    for c in range(CHANS):
+        here = ref[pl.ds(first + c * STEP, 8), :]
+        before = ref[pl.ds(first + c * STEP - 1, 8), :]
+        moved = pltpu.roll(jnp.where(keep, here, before), turn, 1)
+        total[c] = moved if total[c] is None else total[c] + moved
+
+
+def fleet_of(shot):
+    return ((shot + 1) >> 9) & 1
+
+
+def residual_kernel(lag_ref, dat_ref, est_ref, res, part, tmp, est):
     place = lax.axis_index("shot")
     est[...] = jnp.zeros_like(est)
     res[...] = jnp.zeros_like(res)
-    upd[1024:, :] = jnp.zeros((1024, 128), jnp.float32)
+    part[1024:, :] = jnp.zeros((512, 128), jnp.float32)
     tmp[...] = est_ref[...].astype(jnp.float32)
-
-    def base(row, c):
-        return (row * CHANS + c) * STEP + 16
-
     for c in range(CHANS):
         for u in range(8):
             columns = slice(128 * u, 128 * u + 128)
             old = tmp[:, c, columns]
             est[pl.ds(base(2, c) + u, BLOCK, stride=CHANS * STEP), :] = old
             res[pl.ds(base(3, c) + u, BLOCK, stride=CHANS * STEP), :] = dat_ref[:, c, columns] - old
-
     lanes = lane_ids(8)
-
-    def companions(ref, row_of, side, n, kinds):
-        shot = (512 * side + BLOCK * place + n + SHOTS) & (SHOTS - 1)
-        fleet = ((shot + 1) >> 9) & 1
-        own = (shot & 15) * 6 + 3 * fleet
-        other = (shot & 15) * 6 + 3 - 3 * fleet
-        slots = ((own, 0, -1), (own + 2, 0, 1), (other, 1, -1), (other + 1, 1, 0), (other + 2, 1, 1))
-        total = [None] * CHANS
-        for at, flip, step in slots:
-            if flip not in kinds:
-                continue
-            lag = lag_ref[shot >> 4, at]
-            turn = lag & 127
-            keep = lanes < 128 - turn
-            first = base(row_of(side ^ flip, n + step), 0) - (lag >> 7)
-            for c in range(CHANS):
-                here = ref[pl.ds(first + c * STEP, 8), :]
-                before = ref[pl.ds(first + c * STEP - 1, 8), :]
-                moved = pltpu.roll(jnp.where(keep, here, before), turn, 1)
-                total[c] = moved if total[c] is None else total[c] + moved
-        return total
-
-    def est_row(side, n):
-        return n + 2
-
-    def res_row(side, n):
-        return side * 22 + n + 3
 
     @pl.loop(0, BLOCK + 2)
     def _(step):
         n = step - 1
-        near = companions(est, est_row, 0, n, (0,))
-        far = companions(est, est_row, 1, n, (1,))
-        for c in range(CHANS):
-            rows = pl.ds(base(res_row(0, n), c), 8)
-            res[rows, :] = res[rows, :] - near[c]
-            res[pl.ds(base(res_row(1, n), c), 8), :] = -far[c]
+        for side in range(2):
+            total = [None] * CHANS
+            for ahead in (-1, 1) if side == 0 else (-1, 0, 1):
+                m = jnp.clip(n + ahead, 0, BLOCK - 1)
+                fleet = fleet_of(BLOCK * place + m)
+                lag = -lag_ref[m * 6 + 3 * (fleet ^ side) + 1 - ahead]
+                add_shifted(total, est, base(n + ahead + 2, 0), lag, lanes)
+            for c in range(CHANS):
+                rows = pl.ds(base(res_row(side, n), c), 8)
+                value = -total[c] if side else res[rows, :] - total[c]
+                res[rows, :] = value
+                value = 0.25 * value
+                if side == 0:
+                    value = value + est[pl.ds(base(n + 2, c), 8), :]
+                part[pl.ds((place_of(side, n) + c * BLOCK) * 8, 8), :] = value
+
+
+def blend_kernel(lag_ref, res, part, table_hbm, out_ref, upd, acc, table, sem):
+    copy = pltpu.make_async_copy(table_hbm, table, sem)
+    copy.start()
+    place = lax.axis_index("shot")
+    upd[1024:, :] = jnp.zeros((1024, 128), jnp.float32)
+    lanes = lane_ids(8)
 
     @pl.loop(0, BLOCK + 4)
     def _(step):
         n = step - 2
         for side in range(2):
-            total = companions(res, res_row, side, n, (0, 1))
-            low = 128 + (14 if side == 0 else 12) + n + 2
-            high = 128 + (0 if side == 0 else 2) + n - 16
-            at = jnp.where(n < 0, low, jnp.where(n > 15, high, side * 64 + n))
+            shot = (512 * side + BLOCK * place + n + SHOTS) & (SHOTS - 1)
+            fleet = fleet_of(shot)
+            total = [None] * CHANS
+            for flip, ahead in ((0, -1), (0, 1), (1, -1), (1, 0), (1, 1)):
+                lag = lag_ref[shot >> 4, (shot & 15) * 6 + 3 * (fleet ^ flip) + 1 + ahead]
+                add_shifted(total, res, base(res_row(side ^ flip, n + ahead), 0), lag, lanes)
             for c in range(CHANS):
-                value = 0.25 * (total[c] + res[pl.ds(base(res_row(side, n), c), 8), :])
-                if side == 0:
-                    value = value + est[pl.ds(base(n + 2, c), 8), :]
-                upd[pl.ds((at + c * BLOCK) * 8, 8), :] = value
+                rows = pl.ds((place_of(side, n) + c * BLOCK) * 8, 8)
+                upd[rows, :] = part[rows, :] + 0.25 * total[c]
 
     rows = jnp.concatenate([upd[pl.ds(u, 256, stride=8), :] for u in range(8)], 1).astype(jnp.bfloat16)
     copy.wait()
@@ -146,7 +158,7 @@
     out_ref[...] = acc[...].reshape(DEVS * 24, 128).astype(jnp.bfloat16)
 
 
-def forward_kernel(x_ref, place_ref, turn_ref, block_ref, spec_ref, peak_ref, tmp):
+def forward_kernel(level_ref, x_ref, place_ref, turn_ref, block_ref, spec_ref, limit_ref, tmp):
     x = x_ref[...].astype(jnp.float32).reshape(DEVS, 24, 128)
     real, imag, rims = x[:, :8], x[:, 8:16], x[:, 16:]
 
@@ -186,12 +198,12 @@
     )
     for shift in (1, 2, 4, 8, 16, 32):
         peak = jnp.maximum(peak, pltpu.roll(peak, shift, 1))
-    peak_ref[...] = jnp.broadcast_to(peak[None], peak_ref.shape)
-
-
-def backward_kernel(level_ref, spec_ref, peak_ref, place_ref, turn_ref, block_ref, out_ref, tmp):
-    peak = jnp.sqrt(jnp.max(peak_ref[...], axis=0))
-    limit = level_ref[0].astype(jnp.float32) * (1 / 64) * (peak + 1e-6)
+    limit = level_ref[0].astype(jnp.float32) * (1 / 64) * (jnp.sqrt(peak) + 1e-6)
+    limit_ref[...] = jnp.broadcast_to(limit[None], limit_ref.shape)
+
+
+def backward_kernel(spec_ref, limit_ref, place_ref, turn_ref, block_ref, out_ref, tmp):
+    limit = jnp.max(limit_ref[...], axis=0)
     shrunk = []
     for kk in range(8):
         value = spec_ref[64 * kk : 64 * kk + 64, :]
@@ -233,7 +245,7 @@
     return pl.BlockSpec(memory_space=pltpu.SMEM)
 
 
-def call(kernel, outs, in_specs, scratch=()):
+def call(kernel, outs, in_specs, scratch=(), cost=None):
     return pl.pallas_call(
         kernel,
         out_shape=outs,
@@ -241,42 +253,53 @@
         out_specs=vmem(len(outs)) if isinstance(outs, list) else vmem(1)[0],
         scratch_shapes=list(scratch),
         compiler_params=pltpu.CompilerParams(vmem_limit_bytes=32 * 1024 * 1024),
+        cost_estimate=cost,
         interpret=INTERPRET,
     )
 
 
 def local(blended, estimate, neighbour_sources, partner_lags, threshold_level):
     lags = jnp.pad(partner_lags.reshape(-1), (0, 32))
-    lags = lax.all_to_all(jnp.broadcast_to(lags, (DEVS, 128)), "shot", 0, 0, tiled=True)
+    all_lags = lax.all_to_all(jnp.broadcast_to(lags, (DEVS, 128)), "shot", 0, 0, tiled=True)
+    res, part = call(
+        residual_kernel,
+        [
+            jax.ShapeDtypeStruct((44 * CHANS * STEP + 16, 128), jnp.float32),
+            jax.ShapeDtypeStruct((192 * 8, 128), jnp.float32),
+        ],
+        [smem()] + vmem(2),
+        [
+            pltpu.VMEM((BLOCK, CHANS, SAMPLES), jnp.float32),
+            pltpu.VMEM((20 * CHANS * STEP + 16, 128), jnp.float32),
+        ],
+        pl.CostEstimate(flops=4_000_000, bytes_accessed=16_000_000, transcendentals=0),
+    )(lags, blended, estimate)
     send = call(
         blend_kernel,
         jax.ShapeDtypeStruct((DEVS * 24, 128), jnp.bfloat16),
         [smem()] + vmem(2) + [pl.BlockSpec(memory_space=pl.ANY)],
         [
-            pltpu.VMEM((BLOCK, CHANS, SAMPLES), jnp.float32),
-            pltpu.VMEM((20 * CHANS * STEP + 16, 128), jnp.float32),
-            pltpu.VMEM((44 * CHANS * STEP + 16, 128), jnp.float32),
             pltpu.VMEM((2048, 128), jnp.float32),
             pltpu.VMEM((DEVS, 24, 128), jnp.float32),
             pltpu.VMEM((SAMPLES, SAMPLES), jnp.bfloat16),
             pltpu.SemaphoreType.DMA,
         ],
-    )(lags, blended, estimate, time_table())
+    )(all_lags, res, part, time_table())
     columns = lax.all_to_all(send.reshape(DEVS, 24, 128), "shot", 0, 0, tiled=True).reshape(DEVS * 24, 128)
     others = lax.axis_size("chan")
-    spec, peak = call(
+    spec, limit = call(
         forward_kernel,
         [jax.ShapeDtypeStruct((512, 128), jnp.float32), jax.ShapeDtypeStruct((others, 8, 128), jnp.float32)],
-        vmem(4),
+        [smem()] + vmem(4),
         [pltpu.VMEM((512, 128), jnp.float32)],
-    )(columns, place_table(), twiddles(), block_table(-1))
-    peaks = lax.all_to_all(peak, "chan", 0, 0, tiled=True)
+    )(threshold_level, columns, place_table(), twiddles(), block_table(-1))
+    limits = lax.all_to_all(limit, "chan", 0, 0, tiled=True)
     back = call(
         backward_kernel,
         jax.ShapeDtypeStruct((512, 128), jnp.bfloat16),
-        [smem()] + vmem(5),
+        vmem(5),
         [pltpu.VMEM((512, 128), jnp.float32)],
-    )(threshold_level, spec, peaks, place_table(), twiddles(), block_table(1))
+    )(spec, limits, place_table(), twiddles(), block_table(1))
     arrived = lax.all_to_all(back.reshape(DEVS, 8, 128), "shot", 0, 0, tiled=True).reshape(512, 128)
     return call(
         time_back_kernel,

time: 90.6 us -> 88.9 us (0.981)
  blocking collectives: 61 us -> 31.4 us
  starting transfers between devices: 6.81 us -> 21 us
  waiting for transfers between devices: 6.25 us -> 18.7 us
    all_to_all x2 -> x1, blocking collectives: 43.1 us -> 13.5 us  [local(): limits = lax.all_to_all(limit, 'chan', 0, 0, tiled=True)]
    all_to_all x1 -> x2, starting transfers between devices: 6.81 us -> 21 us  [the longest x1 14.8 us: local(): lax.all_to_all(jnp.broadcast_to(lags, (DEVS, 128)), 'shot', 0, 0, tiled=T...]
    all_to_all x1 -> x2, waiting for transfers between devices: 6.25 us -> 18.7 us  [the longest x1 14.4 us: local(): lax.all_to_all(send.reshape(DEVS, 24, 128), 'shot', 0, 0, tiled=True)]
    pallas_call x1 -> x2, Pallas kernels: 0.65 us -> 3.76 us  [the longest x1 3.11 us: local(): call(residual_kernel, [jax.ShapeDtypeStruct((44 * CHANS * STEP + 16, 128)...]
    pallas_call x1, Pallas kernels: 7.25 us -> 5.44 us  [local(): call(blend_kernel, jax.ShapeDtypeStruct((DEVS * 24, 128), jnp.bfloat16),...]
  transfers between devices with their start and end apart: 1 -> 2, of which waited for: 1 -> 2; matrix products, arithmetic and copies ran while one was open for 0% -> 0% of each run, Pallas kernels for 0% -> 4%
where the time goes in v3:
time: 88.9 us; the launch traced here: 88.5 us
  blocking collectives  31.4 us (35%)
  starting transfers between devices  21 us (24%)
  waiting for transfers between devices  18.7 us (21%)
  Pallas kernels  11.7 us (13%)
  local copies, waits for them, and re-layouts  4.95 us (6%)
    all_to_all x1, blocking collectives, local(): lax.all_to_all(back.reshape(DEVS, 8, 128), 'shot', 0, 0, tiled=True)  17.9 us
    all_to_all x1, starting transfers between devices, local(): lax.all_to_all(jnp.broadcast_to(lags, (DEVS, 128)), 'shot', 0, 0, tiled=T...  14.8 us
    all_to_all x1, waiting for transfers between devices, local(): lax.all_to_all(send.reshape(DEVS, 24, 128), 'shot', 0, 0, tiled=True)  14.4 us
    all_to_all x1, blocking collectives, local(): limits = lax.all_to_all(limit, 'chan', 0, 0, tiled=True)  13.5 us
    all_to_all x1, starting transfers between devices, local(): lax.all_to_all(send.reshape(DEVS, 24, 128), 'shot', 0, 0, tiled=True)  6.14 us
    pallas_call x1, Pallas kernels, local(): call(blend_kernel, jax.ShapeDtypeStruct((DEVS * 24, 128), jnp.bfloat16),...  5.44 us
    all_to_all x1, waiting for transfers between devices, local(): lax.all_to_all(jnp.broadcast_to(lags, (DEVS, 128)), 'shot', 0, 0, tiled=T...  4.33 us
    unnamed x17, local copies, waits for them, and re-layouts  4.22 us
  transfers between devices with their start and end apart: 2, of which 2 were waited for; matrix products, arithmetic and copies ran while one was open for 0% of the time, Pallas kernels for 4%

profile of v3, /device:TPU:1, one launch (start us, length us, event | category | flops | bytes accessed | tf_op | source)
XLA Modules:
  0.0 88.5 jit_solution(7978047918163486281)
XLA Ops:
  0.0 0.8 copy.15
  0.8 0.1 reshape.19
  0.9 0.6 broadcast_in_dim.3
  1.5 14.8 %all-to-all-start = ((s32[64,1,128]{2,1,0:T(1,128)}), s32[64,1,128]{2,1,0:T(1,128)S(1)}, u32[]{:S(2)}, u32[]{:S(2)}) async-start(s32[64,1,128]{2,1,0:T(1,128)} %broadcast_in_dim.3), calls=%async_computation | async-start | bytes 65536 | tf_op jit(solution)/shard_map/all_to_all | solution.py:263
  16.3 0.0 copy-start.3
  16.4 0.9 %copy-done.3 = f32[16,4,1024]{2,1,0:T(4,128)S(1)} copy-done((f32[16,4,1024]{2,1,0:T(4,128)S(1)}, f32[16,4,1024]{2,1,0:T(4,128)}, u32[]{:S(2)}) %copy-start.3) | copy-done | bytes 262168
  17.3 0.0 copy-start.5
  17.3 0.9 %copy-done.5 = bf16[16,4,1024]{2,1,0:T(4,128)(2,1)S(1)} copy-done((bf16[16,4,1024]{2,1,0:T(4,128)(2,1)S(1)}, bf16[16,4,1024]{2,1,0:T(4,128)(2,1)}, u32[]{:S(2)}) %copy-start.5) | copy-done | bytes 131096
  18.2 3.1 %shard_map.118 = (f32[4240,128]{1,0:T(8,128)S(1)}, f32[1536,128]{1,0:T(8,128)S(1)}) custom-call(s32[128]{0:T(128)S(1)} %pad.4.lag_ref, f32[16,4,1024]{2,1,0:T(4,128)S(1)} %copy-done.3, bf16[16,4,1024]{2,1,0:T(4,128)(2,1)S(1)} %copy-done.5), custom_call_target="tpu_custom_call" | custom-call | flops 4000000 | bytes 16000000 | tf_op jit(solution)/shard_map/pallas_call | solution.py:264
  21.3 4.3 %all-to-all-done = s32[64,1,128]{2,1,0:T(1,128)S(1)} async-done(((s32[64,1,128]{2,1,0:T(1,128)}), s32[64,1,128]{2,1,0:T(1,128)S(1)}, u32[]{:S(2)}, u32[]{:S(2)}) %all-to-all-start) | async-done | bytes 32800 | tf_op jit(solution)/shard_map/all_to_all | solution.py:263
  25.6 0.0 copy-start.1
  25.6 1.6 %copy-done.1 = bf16[1024,1024]{1,0:T(8,128)(2,1)S(1)} copy-done((bf16[1024,1024]{1,0:T(8,128)(2,1)S(1)}, bf16[1024,1024]{1,0:T(8,128)(2,1)}, u32[]{:S(2)}) %copy-start.1) | copy-done | bytes 2097176
  27.2 0.0 copy-start.2
  27.2 0.0 copy-start.4
  27.2 0.0 copy-start.7
  27.2 0.0 copy-start.6
  27.2 5.4 %shard_map.119 = bf16[1536,128]{1,0:T(8,128)(2,1)} custom-call(s32[64,128]{1,0:T(8,128)S(1)} %bitcast.8, f32[4240,128]{1,0:T(8,128)S(1)} %get-tuple-element.9.res, f32[1536,128]{1,0:T(8,128)S(1)} %get-tuple-element.10.part, bf16[1024,1024]{1,0:T(8,128)(2,1)S(1)} %copy-done.1), custom_call_target="tpu_custom_call" | custom-call | tf_op jit(solution)/shard_map/pallas_call | solution.py:277
  32.7 0.0 copy-start
  32.7 6.1 %all-to-all-start.1 = ((bf16[64,24,128]{2,1,0:T(8,128)(2,1)}), bf16[64,24,128]{2,1,0:T(8,128)(2,1)S(1)}, u32[]{:S(2)}, u32[]{:S(2)}) async-start(bf16[64,24,128]{2,1,0:T(8,128)(2,1)} %bitcast.1), calls=%async_computation.1 | async-start | bytes 786432 | tf_op jit(solution)/shard_map/all_to_all | solution.py:288
  39.5 14.4 %all-to-all-done.1 = bf16[64,24,128]{2,1,0:T(8,128)(2,1)S(1)} async-done(((bf16[64,24,128]{2,1,0:T(8,128)(2,1)}), bf16[64,24,128]{2,1,0:T(8,128)(2,1)S(1)}, u32[]{:S(2)}, u32[]{:S(2)}) %all-to-all-start.1) | async-done | bytes 393248 | tf_op jit(solution)/shard_map/all_to_all | solution.py:288
  53.9 0.0 copy-done.2
  53.9 0.0 copy-done.4
  53.9 0.0 copy-done.7
  53.9 1.3 %shard_map.120 = (f32[512,128]{1,0:T(8,128)S(1)}, f32[8,8,128]{2,1,0:T(8,128)S(1)}) custom-call(s32[1]{0:T(128)S(6)} %copy.16.level_ref, bf16[1536,128]{1,0:T(8,128)(2,1)S(1)} %bitcast.5, bf16[128,64]{1,0:T(8,128)(2,1)S(1)} %copy-done.4, f32[64,256]{1,0:T(8,128)S(1)} %copy-done.2, bf16[128,128]{1,0:T(8,128)(2,1)S(1)} %copy-done.7), custom_call_target="tpu_custom_call" | custom-call | tf_op jit(solution)/shard_map/pallas_call | solution.py:290
  55.2 13.5 %all_to_all.23.limit_ref = f32[8,8,128]{2,1,0:T(8,128)S(1)} all-to-all(f32[8,8,128]{2,1,0:T(8,128)S(1)} %get-tuple-element.12), channel_id=1, replica_groups=mesh['shot'=64,'chan'=8] {'chan'}, dimensions={0} | all-to-all | bytes 65536 | tf_op jit(solution)/shard_map/all_to_all | solution.py:296
  68.7 0.0 copy-done.6
  68.7 0.6 shard_map.121
  69.3 17.9 %all_to_all.24 = bf16[64,8,128]{2,1,0:T(8,128)(2,1)S(1)} all-to-all(bf16[64,8,128]{2,1,0:T(8,128)(2,1)S(1)} %bitcast.6), channel_id=1, replica_groups=mesh['shot'=64,'chan'=8] {'shot'}, dimensions={0} | all-to-all | bytes 262144 | tf_op jit(solution)/shard_map/all_to_all | solution.py:303
  87.3 0.0 copy-done
  87.3 1.3 %shard_map.122 = f32[16,4,1024]{2,1,0:T(4,128)} custom-call(bf16[512,128]{1,0:T(8,128)(2,1)S(1)} %bitcast.7, bf16[1024,1024]{1,0:T(8,128)(2,1)S(1)} %copy-done), custom_call_target="tpu_custom_call" | custom-call | tf_op jit(solution)/shard_map/pallas_call | solution.py:304
  (1 shorter events, 0.0 us)
Async XLA Ops:
  1.5 24.1 %all-to-all-start = ((s32[64,1,128]{2,1,0:T(1,128)}), s32[64,1,128]{2,1,0:T(1,128)S(1)}, u32[]{:S(2)}, u32[]{:S(2)}) async-start(s32[64,1,128]{2,1,0:T(1,128)} %broadcast_in_dim.3), calls=%async_computation | async-start | bytes 65536 | tf_op jit(solution)/shard_map/all_to_all | solution.py:263
  16.3 1.0 %copy-start.3 = (f32[16,4,1024]{2,1,0:T(4,128)S(1)}, f32[16,4,1024]{2,1,0:T(4,128)}, u32[]{:S(2)}) copy-start(f32[16,4,1024]{2,1,0:T(4,128)} %dat_ref.1) | copy-start | bytes 786436
  17.3 0.9 %copy-start.5 = (bf16[16,4,1024]{2,1,0:T(4,128)(2,1)S(1)}, bf16[16,4,1024]{2,1,0:T(4,128)(2,1)}, u32[]{:S(2)}) copy-start(bf16[16,4,1024]{2,1,0:T(4,128)(2,1)} %est_ref.1) | copy-start | bytes 393220
  25.6 1.6 %copy-start.1 = (bf16[1024,1024]{1,0:T(8,128)(2,1)S(1)}, bf16[1024,1024]{1,0:T(8,128)(2,1)}, u32[]{:S(2)}) copy-start(bf16[1024,1024]{1,0:T(8,128)(2,1)} %constant.14.clone.table_hbm) | copy-start | bytes 6291460
  27.2 26.7 %copy-start.2 = (f32[64,256]{1,0:T(8,128)S(1)}, f32[64,256]{1,0:T(8,128)}, u32[]{:S(2)}) copy-start(f32[64,256]{1,0:T(8,128)} %constant.16.clone.turn_ref) | copy-start | bytes 196612
  27.2 26.7 %copy-start.4 = (bf16[128,64]{1,0:T(8,128)(2,1)S(1)}, bf16[128,64]{1,0:T(8,128)(2,1)}, u32[]{:S(2)}) copy-start(bf16[128,64]{1,0:T(8,128)(2,1)} %constant.15.clone.place_ref) | copy-start | bytes 49156
  27.2 26.7 %copy-start.7 = (bf16[128,128]{1,0:T(8,128)(2,1)S(1)}, bf16[128,128]{1,0:T(8,128)(2,1)}, u32[]{:S(2)}) copy-start(bf16[128,128]{1,0:T(8,128)(2,1)} %constant.17.clone.block_ref) | copy-start | bytes 98308
  27.2 41.4 %copy-start.6 = (bf16[128,128]{1,0:T(8,128)(2,1)S(1)}, bf16[128,128]{1,0:T(8,128)(2,1)}, u32[]{:S(2)}) copy-start(bf16[128,128]{1,0:T(8,128)(2,1)} %constant.18.clone.block_ref) | copy-start | bytes 98308
  32.7 54.6 %copy-start = (bf16[1024,1024]{1,0:T(8,128)(2,1)S(1)}, bf16[1024,1024]{1,0:T(8,128)(2,1)}, u32[]{:S(2)}) copy-start(bf16[1024,1024]{1,0:T(8,128)(2,1)} %constant.19.clone.table_ref) | copy-start | bytes 6291460
  32.7 21.2 %all-to-all-start.1 = ((bf16[64,24,128]{2,1,0:T(8,128)(2,1)}), bf16[64,24,128]{2,1,0:T(8,128)(2,1)S(1)}, u32[]{:S(2)}, u32[]{:S(2)}) async-start(bf16[64,24,128]{2,1,0:T(8,128)(2,1)} %bitcast.1), calls=%async_computation.1 | async-start | bytes 786432 | tf_op jit(solution)/shard_map/all_to_all | solution.py:288

commit v4 on v3

--- a/solution.py
+++ b/solution.py
@@ -12,19 +12,27 @@
 INTERPRET = False
 
 
+def half_phases(parity):
+    k = 2 * np.arange(FREQS // 2)[:, None] + parity
+    t = np.arange(SAMPLES // 2)[None, :]
+    return k, 2 * np.pi * ((t * k) % SAMPLES) / SAMPLES
+
+
 def time_table():
-    t = np.arange(SAMPLES)[None, :]
-    k = np.arange(FREQS)[:, None]
-    phase = 2 * np.pi * ((t * k) % SAMPLES) / SAMPLES
-    return (np.concatenate([np.cos(phase), -np.sin(phase)], 0) / 32).astype(jnp.bfloat16)
+    parts = []
+    for parity in range(2):
+        _, phase = half_phases(parity)
+        parts += [np.cos(phase) / 32, -np.sin(phase) / 32]
+    return np.concatenate(parts, 0).astype(jnp.bfloat16)
 
 
 def time_back_table():
-    t = np.arange(SAMPLES)[None, :]
-    k = np.arange(FREQS)[:, None]
-    phase = 2 * np.pi * ((t * k) % SAMPLES) / SAMPLES
-    weight = np.where(k == 0, 1.0, 2.0) / 32
-    return np.concatenate([weight * np.cos(phase), -weight * np.sin(phase)], 0).astype(jnp.bfloat16)
+    parts = []
+    for parity in range(2):
+        k, phase = half_phases(parity)
+        weight = np.where(k == 0, 1.0, 2.0) / 32
+        parts += [weight * np.cos(phase), -weight * np.sin(phase)]
+    return np.concatenate(parts, 0).astype(jnp.bfloat16)
 
 
 def place_table():
@@ -87,8 +95,17 @@
     return ((shot + 1) >> 9) & 1
 
 
-def residual_kernel(lag_ref, dat_ref, est_ref, res, part, tmp, est):
+def lag_kernel(lag_ref, out_ref):
+    own = jnp.pad(lag_ref[...], ((0, 0), (0, 128 - BLOCK)))
+    row = own[0:1]
+    for slot in range(1, 6):
+        row = row + pltpu.roll(own[slot : slot + 1], BLOCK * slot, 1)
+    out_ref[...] = jnp.broadcast_to(row, out_ref.shape)
+
+
+def residual_kernel(level_ref, lag_ref, dat_ref, est_ref, res, part, level_out, tmp, est):
     place = lax.axis_index("shot")
+    level_out[...] = jnp.full((8, 128), level_ref[0].astype(jnp.float32) * (1 / 64))
     est[...] = jnp.zeros_like(est)
     res[...] = jnp.zeros_like(res)
     part[1024:, :] = jnp.zeros((512, 128), jnp.float32)
@@ -101,7 +118,7 @@
             res[pl.ds(base(3, c) + u, BLOCK, stride=CHANS * STEP), :] = dat_ref[:, c, columns] - old
     lanes = lane_ids(8)
 
-    @pl.loop(0, BLOCK + 2)
+    @pl.loop(0, BLOCK + 2, unroll=2)
     def _(step):
         n = step - 1
         for side in range(2):
@@ -109,7 +126,7 @@
             for ahead in (-1, 1) if side == 0 else (-1, 0, 1):
                 m = jnp.clip(n + ahead, 0, BLOCK - 1)
                 fleet = fleet_of(BLOCK * place + m)
-                lag = -lag_ref[m * 6 + 3 * (fleet ^ side) + 1 - ahead]
+                lag = -lag_ref[0, (3 * (fleet ^ side) + 1 - ahead) * BLOCK + m]
                 add_shifted(total, est, base(n + ahead + 2, 0), lag, lanes)
             for c in range(CHANS):
                 rows = pl.ds(base(res_row(side, n), c), 8)
@@ -121,14 +138,12 @@
                 part[pl.ds((place_of(side, n) + c * BLOCK) * 8, 8), :] = value
 
 
-def blend_kernel(lag_ref, res, part, table_hbm, out_ref, upd, acc, table, sem):
-    copy = pltpu.make_async_copy(table_hbm, table, sem)
-    copy.start()
+def blend_kernel(lag_ref, res, part, table, out_ref, upd, acc):
     place = lax.axis_index("shot")
     upd[1024:, :] = jnp.zeros((1024, 128), jnp.float32)
     lanes = lane_ids(8)
 
-    @pl.loop(0, BLOCK + 4)
+    @pl.loop(0, BLOCK + 4, unroll=4)
     def _(step):
         n = step - 2
         for side in range(2):
@@ -136,25 +151,24 @@
             fleet = fleet_of(shot)
             total = [None] * CHANS
             for flip, ahead in ((0, -1), (0, 1), (1, -1), (1, 0), (1, 1)):
-                lag = lag_ref[shot >> 4, (shot & 15) * 6 + 3 * (fleet ^ flip) + 1 + ahead]
+                lag = lag_ref[shot >> 4, (3 * (fleet ^ flip) + 1 + ahead) * BLOCK + (shot & 15)]
                 add_shifted(total, res, base(res_row(side ^ flip, n + ahead), 0), lag, lanes)
             for c in range(CHANS):
                 rows = pl.ds((place_of(side, n) + c * BLOCK) * 8, 8)
                 upd[rows, :] = part[rows, :] + 0.25 * total[c]
 
-    rows = jnp.concatenate([upd[pl.ds(u, 256, stride=8), :] for u in range(8)], 1).astype(jnp.bfloat16)
-    copy.wait()
-    rims = None
-    for ri in range(2):
+    octaves = [upd[pl.ds(u, 256, stride=8), :] for u in range(8)]
+    for parity in range(2):
+        rows = [octaves[u] - octaves[u + 4] if parity else octaves[u] + octaves[u + 4] for u in range(4)]
         product = lax.dot_general(
-            table[512 * ri : 512 * ri + 512, :],
-            rows,
+            table[512 * parity : 512 * parity + 512, :],
+            jnp.concatenate(rows, 1).astype(jnp.bfloat16),
             (((1,), (1,)), ((), ())),
             preferred_element_type=jnp.float32,
         )
-        acc[:, 8 * ri : 8 * ri + 8, :] = product[:, :128].reshape(DEVS, 8, 128)
-        rims = product[:, 128:] if rims is None else rims + swapped(product[:, 128:])
-    acc[:, 16:24, :] = rims.reshape(DEVS, 8, 128)
+        real, imag = product[:256], product[256:]
+        for at, value in ((0, real[:, :128]), (8, imag[:, :128]), (16, real[:, 128:] + swapped(imag[:, 128:]))):
+            acc[:, parity, at : at + 8, :] = value.reshape(DEVS // 2, 8, 128)
     out_ref[...] = acc[...].reshape(DEVS * 24, 128).astype(jnp.bfloat16)
 
 
@@ -198,7 +212,7 @@
     )
     for shift in (1, 2, 4, 8, 16, 32):
         peak = jnp.maximum(peak, pltpu.roll(peak, shift, 1))
-    limit = level_ref[0].astype(jnp.float32) * (1 / 64) * (jnp.sqrt(peak) + 1e-6)
+    limit = level_ref[...] * (jnp.sqrt(peak) + 1e-6)
     limit_ref[...] = jnp.broadcast_to(limit[None], limit_ref.shape)
 
 
@@ -228,13 +242,16 @@
 
 
 def time_back_kernel(x_ref, table_ref, out_ref):
-    turned = x_ref[...].astype(jnp.float32).T.astype(jnp.bfloat16)
-    left = jnp.concatenate([turned[:64], turned[64:]], 1)
-    for n in range(4):
-        columns = slice(256 * n, 256 * n + 256)
-        product = jnp.dot(left, table_ref[:, columns], preferred_element_type=jnp.float32)
+    x = x_ref[...].astype(jnp.float32).reshape(DEVS // 2, 2, 8, 128)
+    halves = []
+    for parity in range(2):
+        turned = x[:, parity].reshape(256, 128).T.astype(jnp.bfloat16)
+        left = jnp.concatenate([turned[:64], turned[64:]], 1)
+        table = table_ref[512 * parity : 512 * parity + 512, :]
+        halves.append(jnp.dot(left, table, preferred_element_type=jnp.float32))
+    for half, value in enumerate((halves[0] + halves[1], halves[0] - halves[1])):
         for c in range(CHANS):
-            out_ref[:, c, columns] = product[BLOCK * c : BLOCK * c + BLOCK]
+            out_ref[:, c, 512 * half : 512 * half + 512] = value[BLOCK * c : BLOCK * c + BLOCK]
 
 
 def vmem(count):
@@ -252,47 +269,43 @@
         in_specs=in_specs,
         out_specs=vmem(len(outs)) if isinstance(outs, list) else vmem(1)[0],
         scratch_shapes=list(scratch),
-        compiler_params=pltpu.CompilerParams(vmem_limit_bytes=32 * 1024 * 1024),
+        compiler_params=pltpu.CompilerParams(vmem_limit_bytes=8 * 1024 * 1024),
         cost_estimate=cost,
         interpret=INTERPRET,
     )
 
 
 def local(blended, estimate, neighbour_sources, partner_lags, threshold_level):
-    lags = jnp.pad(partner_lags.reshape(-1), (0, 32))
-    all_lags = lax.all_to_all(jnp.broadcast_to(lags, (DEVS, 128)), "shot", 0, 0, tiled=True)
-    res, part = call(
+    own_lags = call(lag_kernel, jax.ShapeDtypeStruct((DEVS, 128), jnp.int32), vmem(1))(partner_lags.T)
+    all_lags = lax.all_to_all(own_lags, "shot", 0, 0, tiled=True)
+    res, part, level = call(
         residual_kernel,
         [
             jax.ShapeDtypeStruct((44 * CHANS * STEP + 16, 128), jnp.float32),
             jax.ShapeDtypeStruct((192 * 8, 128), jnp.float32),
+            jax.ShapeDtypeStruct((8, 128), jnp.float32),
         ],
-        [smem()] + vmem(2),
+        [smem()] * 2 + vmem(2),
         [
             pltpu.VMEM((BLOCK, CHANS, SAMPLES), jnp.float32),
             pltpu.VMEM((20 * CHANS * STEP + 16, 128), jnp.float32),
         ],
         pl.CostEstimate(flops=4_000_000, bytes_accessed=16_000_000, transcendentals=0),
-    )(lags, blended, estimate)
+    )(threshold_level, own_lags, blended, estimate)
     send = call(
         blend_kernel,
         jax.ShapeDtypeStruct((DEVS * 24, 128), jnp.bfloat16),
-        [smem()] + vmem(2) + [pl.BlockSpec(memory_space=pl.ANY)],
-        [
-            pltpu.VMEM((2048, 128), jnp.float32),
-            pltpu.VMEM((DEVS, 24, 128), jnp.float32),
-            pltpu.VMEM((SAMPLES, SAMPLES), jnp.bfloat16),
-            pltpu.SemaphoreType.DMA,
-        ],
+        [smem()] + vmem(3),
+        [pltpu.VMEM((2048, 128), jnp.float32), pltpu.VMEM((DEVS // 2, 2, 24, 128), jnp.float32)],
     )(all_lags, res, part, time_table())
     columns = lax.all_to_all(send.reshape(DEVS, 24, 128), "shot", 0, 0, tiled=True).reshape(DEVS * 24, 128)
     others = lax.axis_size("chan")
     spec, limit = call(
         forward_kernel,
         [jax.ShapeDtypeStruct((512, 128), jnp.float32), jax.ShapeDtypeStruct((others, 8, 128), jnp.float32)],
-        [smem()] + vmem(4),
+        vmem(5),
         [pltpu.VMEM((512, 128), jnp.float32)],
-    )(threshold_level, columns, place_table(), twiddles(), block_table(-1))
+    )(level, columns, place_table(), twiddles(), block_table(-1))
     limits = lax.all_to_all(limit, "chan", 0, 0, tiled=True)
     back = call(
         backward_kernel,

time: 88.9 us -> 86.3 us (0.971)
  blocking collectives: 31.4 us -> 53 us
  waiting for transfers between devices: 18.7 us -> 3.68 us
  starting transfers between devices: 21 us -> 14.8 us
  Pallas kernels: 11.7 us -> 9.82 us
  local copies, waits for them, and re-layouts: 4.95 us -> 3.78 us
    all_to_all x0 -> x1, blocking collectives: none -> 21.6 us  [local(): lax.all_to_all(send.reshape(DEVS, 24, 128), 'shot', 0, 0, tiled=True)]
    all_to_all x2 -> x1, waiting for transfers between devices: 18.7 us -> 3.68 us  [local(): all_lags = lax.all_to_all(own_lags, 'shot', 0, 0, tiled=True)]
    all_to_all x2 -> x1, starting transfers between devices: 21 us -> 14.8 us  [local(): all_lags = lax.all_to_all(own_lags, 'shot', 0, 0, tiled=True)]
    pallas_call x1, Pallas kernels: 5.44 us -> 3 us  [local(): call(blend_kernel, jax.ShapeDtypeStruct((DEVS * 24, 128), jnp.bfloat16),...]
    unnamed x17 -> x18, local copies, waits for them, and re-layouts: 4.22 us -> 3.78 us
  transfers between devices with their start and end apart: 2 -> 1, of which waited for: 2 -> 1; matrix products, arithmetic and copies ran while one was open for 0% -> 0% of each run, Pallas kernels for 4% -> 4%
where the time goes in v4:
time: 86.3 us; the launch traced here: 85.9 us
  blocking collectives  53 us (61%)
  starting transfers between devices  14.8 us (17%)
  Pallas kernels  9.82 us (11%)
  local copies, waits for them, and re-layouts  3.78 us (4%)
  waiting for transfers between devices  3.68 us (4%)
    all_to_all x1, blocking collectives, local(): lax.all_to_all(send.reshape(DEVS, 24, 128), 'shot', 0, 0, tiled=True)  21.6 us
    all_to_all x1, blocking collectives, local(): lax.all_to_all(back.reshape(DEVS, 8, 128), 'shot', 0, 0, tiled=True)  17.9 us
    all_to_all x1, starting transfers between devices, local(): all_lags = lax.all_to_all(own_lags, 'shot', 0, 0, tiled=True)  14.8 us
    all_to_all x1, blocking collectives, local(): limits = lax.all_to_all(limit, 'chan', 0, 0, tiled=True)  13.5 us
    unnamed x18, local copies, waits for them, and re-layouts  3.78 us
    all_to_all x1, waiting for transfers between devices, local(): all_lags = lax.all_to_all(own_lags, 'shot', 0, 0, tiled=True)  3.68 us
    pallas_call x1, Pallas kernels, local(): call(residual_kernel, [jax.ShapeDtypeStruct((44 * CHANS * STEP + 16, 128)...  3.11 us
    pallas_call x1, Pallas kernels, local(): call(blend_kernel, jax.ShapeDtypeStruct((DEVS * 24, 128), jnp.bfloat16),...  3 us
  transfers between devices with their start and end apart: 1, of which 1 were waited for; matrix products, arithmetic and copies ran while one was open for 0% of the time, Pallas kernels for 4%

profile of v4, /device:TPU:1, one launch (start us, length us, event | category | flops | bytes accessed | tf_op | source)
XLA Modules:
  0.0 85.9 jit_solution(16838975953480695868)
XLA Ops:
  0.0 0.0 copy-start.8
  0.0 0.7 copy-done.8
  0.7 0.7 shard_map.118.lag_ref
  1.4 14.8 %all-to-all-start = ((s32[64,1,128]{2,1,0:T(1,128)}), s32[64,1,128]{2,1,0:T(1,128)S(1)}, u32[]{:S(2)}, u32[]{:S(2)}) async-start(s32[64,1,128]{2,1,0:T(1,128)} %bitcast.2), calls=%async_computation | async-start | bytes 65536 | tf_op jit(solution)/shard_map/all_to_all | solution.py:280
  16.9 0.0 copy-start.2
  16.9 0.9 %copy-done.2 = f32[16,4,1024]{2,1,0:T(4,128)S(1)} copy-done((f32[16,4,1024]{2,1,0:T(4,128)S(1)}, f32[16,4,1024]{2,1,0:T(4,128)}, u32[]{:S(2)}) %copy-start.2) | copy-done | bytes 262168
  17.8 0.0 copy-start.5
  17.8 0.9 %copy-done.5 = bf16[16,4,1024]{2,1,0:T(4,128)(2,1)S(1)} copy-done((bf16[16,4,1024]{2,1,0:T(4,128)(2,1)S(1)}, bf16[16,4,1024]{2,1,0:T(4,128)(2,1)}, u32[]{:S(2)}) %copy-start.5) | copy-done | bytes 131096
  18.7 3.1 %shard_map.119 = (f32[4240,128]{1,0:T(8,128)S(1)}, f32[1536,128]{1,0:T(8,128)S(1)}, f32[8,128]{1,0:T(8,128)S(1)}) custom-call(s32[1]{0:T(128)S(6)} %copy.14.level_ref, s32[64,128]{1,0:T(8,128)} %shard_map.118.lag_ref, f32[16,4,1024]{2,1,0:T(4,128)S(1)} %copy-done.2, bf16[16,4,1024]{2,1,0:T(4,128)(2,1)S(1)} %copy-done.5), custom_call_target="tpu_custom_call" | custom-call | flops 4000000 | bytes 16000000 | tf_op jit(solution)/shard_map/pallas_call | solution.py:281
  21.8 3.7 %all-to-all-done = s32[64,1,128]{2,1,0:T(1,128)S(1)} async-done(((s32[64,1,128]{2,1,0:T(1,128)}), s32[64,1,128]{2,1,0:T(1,128)S(1)}, u32[]{:S(2)}, u32[]{:S(2)}) %all-to-all-start) | async-done | bytes 32800 | tf_op jit(solution)/shard_map/all_to_all | solution.py:280
  25.5 0.0 copy-start.1
  25.5 1.2 %copy-done.1 = bf16[1024,512]{1,0:T(8,128)(2,1)S(1)} copy-done((bf16[1024,512]{1,0:T(8,128)(2,1)S(1)}, bf16[1024,512]{1,0:T(8,128)(2,1)}, u32[]{:S(2)}) %copy-start.1) | copy-done | bytes 1048600
  26.8 0.0 copy-start.3
  26.8 0.0 copy-start.4
  26.8 0.0 copy-start.7
  26.8 0.0 copy-start.6
  26.8 3.0 %shard_map.120 = bf16[1536,128]{1,0:T(8,128)(2,1)S(1)} custom-call(s32[64,128]{1,0:T(8,128)S(1)} %bitcast.13, f32[4240,128]{1,0:T(8,128)S(1)} %get-tuple-element.11.res, f32[1536,128]{1,0:T(8,128)S(1)} %get-tuple-element.12.part, bf16[1024,512]{1,0:T(8,128)(2,1)S(1)} %copy-done.1), custom_call_target="tpu_custom_call" | custom-call | tf_op jit(solution)/shard_map/pallas_call | solution.py:295
  29.8 0.0 copy-start
  29.8 21.6 %all_to_all.26 = bf16[64,24,128]{2,1,0:T(8,128)(2,1)S(1)} all-to-all(bf16[64,24,128]{2,1,0:T(8,128)(2,1)S(1)} %bitcast.10), channel_id=1, replica_groups=mesh['shot'=64,'chan'=8] {'shot'}, dimensions={0} | all-to-all | bytes 786432 | tf_op jit(solution)/shard_map/all_to_all | solution.py:301
  51.4 0.0 copy-done.3
  51.4 0.0 copy-done.4
  51.4 0.0 copy-done.7
  51.4 1.3 %shard_map.121 = (f32[512,128]{1,0:T(8,128)S(1)}, f32[8,8,128]{2,1,0:T(8,128)S(1)}) custom-call(f32[8,128]{1,0:T(8,128)S(1)} %get-tuple-element.10.level_ref, bf16[1536,128]{1,0:T(8,128)(2,1)S(1)} %bitcast.9, bf16[128,64]{1,0:T(8,128)(2,1)S(1)} %copy-done.4, f32[64,256]{1,0:T(8,128)S(1)} %copy-done.3, bf16[128,128]{1,0:T(8,128)(2,1)S(1)} %copy-done.7), custom_call_target="tpu_custom_call" | custom-call | tf_op jit(solution)/shard_map/pallas_call | solution.py:303
  52.7 13.5 %all_to_all.27.limit_ref = f32[8,8,128]{2,1,0:T(8,128)S(1)} all-to-all(f32[8,8,128]{2,1,0:T(8,128)S(1)} %get-tuple-element.14), channel_id=1, replica_groups=mesh['shot'=64,'chan'=8] {'chan'}, dimensions={0} | all-to-all | bytes 65536 | tf_op jit(solution)/shard_map/all_to_all | solution.py:309
  66.2 0.0 copy-done.6
  66.2 0.6 shard_map.122
  66.8 17.9 %all_to_all.28 = bf16[64,8,128]{2,1,0:T(8,128)(2,1)S(1)} all-to-all(bf16[64,8,128]{2,1,0:T(8,128)(2,1)S(1)} %bitcast.11), channel_id=1, replica_groups=mesh['shot'=64,'chan'=8] {'shot'}, dimensions={0} | all-to-all | bytes 262144 | tf_op jit(solution)/shard_map/all_to_all | solution.py:316
  84.8 0.0 copy-done
  84.8 1.1 %shard_map.123 = f32[16,4,1024]{2,1,0:T(4,128)} custom-call(bf16[512,128]{1,0:T(8,128)(2,1)S(1)} %bitcast.12, bf16[1024,512]{1,0:T(8,128)(2,1)S(1)} %copy-done), custom_call_target="tpu_custom_call" | custom-call | tf_op jit(solution)/shard_map/pallas_call | solution.py:317
Async XLA Ops:
  0.0 0.7 copy-start.8
  1.4 24.1 %all-to-all-start = ((s32[64,1,128]{2,1,0:T(1,128)}), s32[64,1,128]{2,1,0:T(1,128)S(1)}, u32[]{:S(2)}, u32[]{:S(2)}) async-start(s32[64,1,128]{2,1,0:T(1,128)} %bitcast.2), calls=%async_computation | async-start | bytes 65536 | tf_op jit(solution)/shard_map/all_to_all | solution.py:280
  16.9 1.0 %copy-start.2 = (f32[16,4,1024]{2,1,0:T(4,128)S(1)}, f32[16,4,1024]{2,1,0:T(4,128)}, u32[]{:S(2)}) copy-start(f32[16,4,1024]{2,1,0:T(4,128)} %dat_ref.1) | copy-start | bytes 786436
  17.8 0.9 %copy-start.5 = (bf16[16,4,1024]{2,1,0:T(4,128)(2,1)S(1)}, bf16[16,4,1024]{2,1,0:T(4,128)(2,1)}, u32[]{:S(2)}) copy-start(bf16[16,4,1024]{2,1,0:T(4,128)(2,1)} %est_ref.1) | copy-start | bytes 393220
  25.5 1.2 %copy-start.1 = (bf16[1024,512]{1,0:T(8,128)(2,1)S(1)}, bf16[1024,512]{1,0:T(8,128)(2,1)}, u32[]{:S(2)}) copy-start(bf16[1024,512]{1,0:T(8,128)(2,1)} %constant.12.clone.table) | copy-start | bytes 3145732
  26.8 24.7 %copy-start.3 = (f32[64,256]{1,0:T(8,128)S(1)}, f32[64,256]{1,0:T(8,128)}, u32[]{:S(2)}) copy-start(f32[64,256]{1,0:T(8,128)} %constant.14.clone.turn_ref) | copy-start | bytes 196612
  26.8 24.7 %copy-start.4 = (bf16[128,64]{1,0:T(8,128)(2,1)S(1)}, bf16[128,64]{1,0:T(8,128)(2,1)}, u32[]{:S(2)}) copy-start(bf16[128,64]{1,0:T(8,128)(2,1)} %constant.13.clone.place_ref) | copy-start | bytes 49156
  26.8 24.7 %copy-start.7 = (bf16[128,128]{1,0:T(8,128)(2,1)S(1)}, bf16[128,128]{1,0:T(8,128)(2,1)}, u32[]{:S(2)}) copy-start(bf16[128,128]{1,0:T(8,128)(2,1)} %constant.15.clone.block_ref) | copy-start | bytes 98308
  26.8 39.4 %copy-start.6 = (bf16[128,128]{1,0:T(8,128)(2,1)S(1)}, bf16[128,128]{1,0:T(8,128)(2,1)}, u32[]{:S(2)}) copy-start(bf16[128,128]{1,0:T(8,128)(2,1)} %constant.16.clone.block_ref) | copy-start | bytes 98308
  29.8 55.0 %copy-start = (bf16[1024,512]{1,0:T(8,128)(2,1)S(1)}, bf16[1024,512]{1,0:T(8,128)(2,1)}, u32[]{:S(2)}) copy-start(bf16[1024,512]{1,0:T(8,128)(2,1)} %constant.17.clone.table_ref) | copy-start | bytes 3145732

commit v5 on v4

--- a/solution.py
+++ b/solution.py
@@ -95,15 +95,9 @@
     return ((shot + 1) >> 9) & 1
 
 
-def lag_kernel(lag_ref, out_ref):
-    own = jnp.pad(lag_ref[...], ((0, 0), (0, 128 - BLOCK)))
-    row = own[0:1]
-    for slot in range(1, 6):
-        row = row + pltpu.roll(own[slot : slot + 1], BLOCK * slot, 1)
-    out_ref[...] = jnp.broadcast_to(row, out_ref.shape)
-
-
-def residual_kernel(level_ref, lag_ref, dat_ref, est_ref, res, part, level_out, tmp, est):
+def residual_kernel(level_ref, all_lags, dat_ref, est_ref, res, part, level_out, tmp, est, lag_ref, sem):
+    copy = pltpu.make_async_copy(all_lags.at[0], lag_ref, sem)
+    copy.start()
     place = lax.axis_index("shot")
     level_out[...] = jnp.full((8, 128), level_ref[0].astype(jnp.float32) * (1 / 64))
     est[...] = jnp.zeros_like(est)
@@ -115,10 +109,11 @@
             columns = slice(128 * u, 128 * u + 128)
             old = tmp[:, c, columns]
             est[pl.ds(base(2, c) + u, BLOCK, stride=CHANS * STEP), :] = old
-            res[pl.ds(base(3, c) + u, BLOCK, stride=CHANS * STEP), :] = dat_ref[:, c, columns] - old
+            res[pl.ds((CHANS + c) * 8 + u, BLOCK, stride=CHANS * 8), :] = dat_ref[:, c, columns] - old
     lanes = lane_ids(8)
-
-    @pl.loop(0, BLOCK + 2, unroll=2)
+    copy.wait()
+
+    @pl.loop(0, BLOCK + 2, unroll=3)
     def _(step):
         n = step - 1
         for side in range(2):
@@ -126,10 +121,10 @@
             for ahead in (-1, 1) if side == 0 else (-1, 0, 1):
                 m = jnp.clip(n + ahead, 0, BLOCK - 1)
                 fleet = fleet_of(BLOCK * place + m)
-                lag = -lag_ref[0, (3 * (fleet ^ side) + 1 - ahead) * BLOCK + m]
+                lag = -lag_ref[(3 * (fleet ^ side) + 1 - ahead) * BLOCK + m]
                 add_shifted(total, est, base(n + ahead + 2, 0), lag, lanes)
             for c in range(CHANS):
-                rows = pl.ds(base(res_row(side, n), c), 8)
+                rows = pl.ds(((side * 18 + step) * CHANS + c) * 8, 8)
                 value = -total[c] if side else res[rows, :] - total[c]
                 res[rows, :] = value
                 value = 0.25 * value
@@ -138,12 +133,25 @@
                 part[pl.ds((place_of(side, n) + c * BLOCK) * 8, 8), :] = value
 
 
-def blend_kernel(lag_ref, res, part, table, out_ref, upd, acc):
+def blend_kernel(all_lags, res_ref, part, out_ref, res, upd, lag_ref, sems):
     place = lax.axis_index("shot")
+    copies = []
+    for number in range(6):
+        source = (place + number % 3 - 1 + 32 * (number // 3) + DEVS) & (DEVS - 1)
+        copies.append(pltpu.make_async_copy(all_lags.at[source], lag_ref.at[number], sems.at[number]))
+        copies[-1].start()
     upd[1024:, :] = jnp.zeros((1024, 128), jnp.float32)
+    res[...] = jnp.zeros_like(res)
+    for side in range(2):
+        for row in range(18):
+            for c in range(CHANS):
+                at = ((side * 18 + row) * CHANS + c) * 8
+                res[pl.ds(base(res_row(side, row - 1), c), 8), :] = res_ref[at : at + 8, :]
     lanes = lane_ids(8)
-
-    @pl.loop(0, BLOCK + 4, unroll=4)
+    for copy in copies:
+        copy.wait()
+
+    @pl.loop(0, BLOCK + 4, unroll=5)
     def _(step):
         n = step - 2
         for side in range(2):
@@ -151,7 +159,7 @@
             fleet = fleet_of(shot)
             total = [None] * CHANS
             for flip, ahead in ((0, -1), (0, 1), (1, -1), (1, 0), (1, 1)):
-                lag = lag_ref[shot >> 4, (3 * (fleet ^ flip) + 1 + ahead) * BLOCK + (shot & 15)]
+                lag = lag_ref[side * 3 + ((n + BLOCK) >> 4), (3 * (fleet ^ flip) + 1 + ahead) * BLOCK + (shot & 15)]
                 add_shifted(total, res, base(res_row(side ^ flip, n + ahead), 0), lag, lanes)
             for c in range(CHANS):
                 rows = pl.ds((place_of(side, n) + c * BLOCK) * 8, 8)
@@ -160,9 +168,14 @@
     octaves = [upd[pl.ds(u, 256, stride=8), :] for u in range(8)]
     for parity in range(2):
         rows = [octaves[u] - octaves[u + 4] if parity else octaves[u] + octaves[u + 4] for u in range(4)]
+        out_ref[256 * parity : 256 * parity + 256, :] = jnp.concatenate(rows, 1).astype(jnp.bfloat16)
+
+
+def time_kernel(rows_ref, table, out_ref, acc):
+    for parity in range(2):
         product = lax.dot_general(
             table[512 * parity : 512 * parity + 512, :],
-            jnp.concatenate(rows, 1).astype(jnp.bfloat16),
+            rows_ref[256 * parity : 256 * parity + 256, :],
             (((1,), (1,)), ((), ())),
             preferred_element_type=jnp.float32,
         )
@@ -276,28 +289,42 @@
 
 
 def local(blended, estimate, neighbour_sources, partner_lags, threshold_level):
-    own_lags = call(lag_kernel, jax.ShapeDtypeStruct((DEVS, 128), jnp.int32), vmem(1))(partner_lags.T)
+    own_lags = jnp.pad(jnp.concatenate([partner_lags[:, slot] for slot in range(6)]), (0, 32))
+    own_lags = jnp.broadcast_to(own_lags, (DEVS, 128))
     all_lags = lax.all_to_all(own_lags, "shot", 0, 0, tiled=True)
     res, part, level = call(
         residual_kernel,
         [
-            jax.ShapeDtypeStruct((44 * CHANS * STEP + 16, 128), jnp.float32),
+            jax.ShapeDtypeStruct((36 * CHANS * 8, 128), jnp.float32),
             jax.ShapeDtypeStruct((192 * 8, 128), jnp.float32),
             jax.ShapeDtypeStruct((8, 128), jnp.float32),
         ],
-        [smem()] * 2 + vmem(2),
+        [smem()] + vmem(3),
         [
             pltpu.VMEM((BLOCK, CHANS, SAMPLES), jnp.float32),
             pltpu.VMEM((20 * CHANS * STEP + 16, 128), jnp.float32),
+            pltpu.SMEM((128,), jnp.int32),
+            pltpu.SemaphoreType.DMA,
         ],
         pl.CostEstimate(flops=4_000_000, bytes_accessed=16_000_000, transcendentals=0),
     )(threshold_level, own_lags, blended, estimate)
+    rows = call(
+        blend_kernel,
+        jax.ShapeDtypeStruct((512, 512), jnp.bfloat16),
+        vmem(3),
+        [
+            pltpu.VMEM((44 * CHANS * STEP + 16, 128), jnp.float32),
+            pltpu.VMEM((2048, 128), jnp.float32),
+            pltpu.SMEM((6, 128), jnp.int32),
+            pltpu.SemaphoreType.DMA((6,)),
+        ],
+    )(all_lags, res, part)
     send = call(
-        blend_kernel,
+        time_kernel,
         jax.ShapeDtypeStruct((DEVS * 24, 128), jnp.bfloat16),
-        [smem()] + vmem(3),
-        [pltpu.VMEM((2048, 128), jnp.float32), pltpu.VMEM((DEVS // 2, 2, 24, 128), jnp.float32)],
-    )(all_lags, res, part, time_table())
+        vmem(2),
+        [pltpu.VMEM((DEVS // 2, 2, 24, 128), jnp.float32)],
+    )(rows, time_table())
     columns = lax.all_to_all(send.reshape(DEVS, 24, 128), "shot", 0, 0, tiled=True).reshape(DEVS * 24, 128)
     others = lax.axis_size("chan")
     spec, limit = call(

time: 86.3 us -> 82.8 us (0.959)
  Pallas kernels: 9.82 us -> 7.34 us
  waiting for transfers between devices: 3.68 us -> 5.96 us
  blocking collectives: 53 us -> 50.9 us
  local copies, waits for them, and re-layouts: 3.78 us -> 2.62 us
    unnamed x18 -> x16, local copies, waits for them, and re-layouts: 3.78 us -> 0.99 us
    pallas_call x3, Pallas kernels: 6.81 us -> 4.34 us  [the longest x1 2.1 us: local(): call(blend_kernel, jax.ShapeDtypeStruct((512, 512), jnp.bfloat16), vmem(3...]
    all_to_all x1, waiting for transfers between devices: 3.68 us -> 5.96 us  [local(): all_lags = lax.all_to_all(own_lags, 'shot', 0, 0, tiled=True)]
    all_to_all x1, blocking collectives: 21.6 us -> 19.3 us  [local(): lax.all_to_all(send.reshape(DEVS, 24, 128), 'shot', 0, 0, tiled=True)]
    squeeze x0 -> x1, local copies, waits for them, and re-layouts: none -> 0.91 us  [local(): partner_lags[:, slot]]
  transfers between devices with their start and end apart: 1 -> 1, of which waited for: 1 -> 1; matrix products, arithmetic and copies ran while one was open for 0% -> 0% of each run, Pallas kernels for 4% -> 2%
where the time goes in v5:
time: 82.8 us; the launch traced here: 82.4 us
  blocking collectives  50.9 us (61%)
  starting transfers between devices  14.8 us (18%)
  Pallas kernels  7.34 us (9%)
  waiting for transfers between devices  5.96 us (7%)
  local copies, waits for them, and re-layouts  2.62 us (3%)
    all_to_all x1, blocking collectives, local(): lax.all_to_all(send.reshape(DEVS, 24, 128), 'shot', 0, 0, tiled=True)  19.3 us
    all_to_all x1, blocking collectives, local(): lax.all_to_all(back.reshape(DEVS, 8, 128), 'shot', 0, 0, tiled=True)  17.9 us
    all_to_all x1, starting transfers between devices, local(): all_lags = lax.all_to_all(own_lags, 'shot', 0, 0, tiled=True)  14.8 us
    all_to_all x1, blocking collectives, local(): limits = lax.all_to_all(limit, 'chan', 0, 0, tiled=True)  13.6 us
    all_to_all x1, waiting for transfers between devices, local(): all_lags = lax.all_to_all(own_lags, 'shot', 0, 0, tiled=True)  5.96 us
    pallas_call x1, Pallas kernels, local(): call(blend_kernel, jax.ShapeDtypeStruct((512, 512), jnp.bfloat16), vmem(3...  2.1 us
    pallas_call x1, Pallas kernels, local(): call(residual_kernel, [jax.ShapeDtypeStruct((36 * CHANS * 8, 128), jnp.fl...  1.7 us
  transfers between devices with their start and end apart: 1, of which 1 were waited for; matrix products, arithmetic and copies ran while one was open for 0% of the time, Pallas kernels for 2%

profile of v5, /device:TPU:1, one launch (start us, length us, event | category | flops | bytes accessed | tf_op | source)
XLA Modules:
  0.0 82.4 jit_solution(876176723960254056)
XLA Ops:
  0.0 0.0 copy-start.5
  0.0 0.9 %slice_bitcast_fusion = (s32[16]{0:T(128)S(1)}, s32[16]{0:T(128)S(1)}, s32[16]{0:T(128)S(1)}, s32[16]{0:T(128)S(1)}, s32[16]{0:T(128)S(1)}, /*index=5*/s32[16]{0:T(128)S(1)}) fusion(s32[16,6]{0,1:T(8,128)} %param.15), kind=kLoop, calls=%fused_computation | loop fusion | bytes 768 | tf_op jit(solution)/shard_map/squeeze | solution.py:292
  0.9 0.1 concatenate.3
  1.0 0.6 broadcast_in_dim.6
  1.6 14.8 %all-to-all-start = ((s32[64,1,128]{2,1,0:T(1,128)}), s32[64,1,128]{2,1,0:T(1,128)S(1)}, u32[]{:S(2)}, u32[]{:S(2)}) async-start(s32[64,1,128]{2,1,0:T(1,128)} %broadcast_in_dim.6), calls=%async_computation | async-start | bytes 65536 | tf_op jit(solution)/shard_map/all_to_all | solution.py:294
  17.1 0.0 copy-done.5
  17.1 0.0 copy-start.2
  17.2 0.9 %copy-done.2 = f32[16,4,1024]{2,1,0:T(4,128)S(1)} copy-done((f32[16,4,1024]{2,1,0:T(4,128)S(1)}, f32[16,4,1024]{2,1,0:T(4,128)}, u32[]{:S(2)}) %copy-start.2) | copy-done | bytes 262168
  18.1 1.7 %shard_map.118 = (f32[1152,128]{1,0:T(8,128)S(1)}, f32[1536,128]{1,0:T(8,128)S(1)}, f32[8,128]{1,0:T(8,128)S(1)}) custom-call(s32[1]{0:T(128)S(6)} %copy.13.level_ref, s32[64,128]{1,0:T(8,128)S(1)} %broadcast_in_dim.5.all_lags, f32[16,4,1024]{2,1,0:T(4,128)S(1)} %copy-done.2, bf16[16,4,1024]{2,1,0:T(4,128)(2,1)S(1)} %copy-done.5), custom_call_target="tpu_custom_call" | custom-call | flops 4000000 | bytes 16000000 | tf_op jit(solution)/shard_map/pallas_call | solution.py:295
  19.8 0.0 copy-start.1
  19.8 6.0 %all-to-all-done = s32[64,1,128]{2,1,0:T(1,128)S(1)} async-done(((s32[64,1,128]{2,1,0:T(1,128)}), s32[64,1,128]{2,1,0:T(1,128)S(1)}, u32[]{:S(2)}, u32[]{:S(2)}) %all-to-all-start) | async-done | bytes 32800 | tf_op jit(solution)/shard_map/all_to_all | solution.py:294
  25.8 2.1 %shard_map.119.rows_ref = bf16[512,512]{1,0:T(8,128)(2,1)S(1)} custom-call(s32[64,128]{1,0:T(8,128)S(1)} %bitcast.21, f32[1152,128]{1,0:T(8,128)S(1)} %get-tuple-element.11.res_ref, f32[1536,128]{1,0:T(8,128)S(1)} %get-tuple-element.12.part), custom_call_target="tpu_custom_call" | custom-call | tf_op jit(solution)/shard_map/pallas_call | solution.py:311
  27.9 0.0 copy-done.1
  27.9 0.0 copy-start.3
  27.9 0.0 copy-start.4
  27.9 0.0 copy-start.7
  27.9 0.5 shard_map.120
  28.5 0.0 copy-start
  28.5 19.3 %all_to_all.23 = bf16[64,24,128]{2,1,0:T(8,128)(2,1)S(1)} all-to-all(bf16[64,24,128]{2,1,0:T(8,128)(2,1)S(1)} %bitcast.18), channel_id=1, replica_groups=mesh['shot'=64,'chan'=8] {'shot'}, dimensions={0} | all-to-all | bytes 786432 | tf_op jit(solution)/shard_map/all_to_all | solution.py:328
  47.8 0.0 copy-done.3
  47.8 0.0 copy-done.4
  47.8 0.0 copy-done.7
  47.8 1.3 %shard_map.121 = (f32[512,128]{1,0:T(8,128)S(1)}, f32[8,8,128]{2,1,0:T(8,128)S(1)}) custom-call(f32[8,128]{1,0:T(8,128)S(1)} %get-tuple-element.10.level_ref, bf16[1536,128]{1,0:T(8,128)(2,1)S(1)} %bitcast.17, bf16[128,64]{1,0:T(8,128)(2,1)S(1)} %copy-done.4, f32[64,256]{1,0:T(8,128)S(1)} %copy-done.3, bf16[128,128]{1,0:T(8,128)(2,1)S(1)} %copy-done.7), custom_call_target="tpu_custom_call" | custom-call | tf_op jit(solution)/shard_map/pallas_call | solution.py:330
  49.1 0.0 copy-start.6
  49.1 13.6 %all_to_all.24.limit_ref = f32[8,8,128]{2,1,0:T(8,128)S(1)} all-to-all(f32[8,8,128]{2,1,0:T(8,128)S(1)} %get-tuple-element.14), channel_id=1, replica_groups=mesh['shot'=64,'chan'=8] {'chan'}, dimensions={0} | all-to-all | bytes 65536 | tf_op jit(solution)/shard_map/all_to_all | solution.py:336
  62.7 0.0 copy-done.6
  62.7 0.6 shard_map.122
  63.4 17.9 %all_to_all.25 = bf16[64,8,128]{2,1,0:T(8,128)(2,1)S(1)} all-to-all(bf16[64,8,128]{2,1,0:T(8,128)(2,1)S(1)} %bitcast.19), channel_id=1, replica_groups=mesh['shot'=64,'chan'=8] {'shot'}, dimensions={0} | all-to-all | bytes 262144 | tf_op jit(solution)/shard_map/all_to_all | solution.py:343
  81.3 0.0 copy-done
  81.3 1.1 %shard_map.123 = f32[16,4,1024]{2,1,0:T(4,128)} custom-call(bf16[512,128]{1,0:T(8,128)(2,1)S(1)} %bitcast.20, bf16[1024,512]{1,0:T(8,128)(2,1)S(1)} %copy-done), custom_call_target="tpu_custom_call" | custom-call | tf_op jit(solution)/shard_map/pallas_call | solution.py:344
  (2 shorter events, 0.0 us)
Async XLA Ops:
  0.0 17.1 %copy-start.5 = (bf16[16,4,1024]{2,1,0:T(4,128)(2,1)S(1)}, bf16[16,4,1024]{2,1,0:T(4,128)(2,1)}, u32[]{:S(2)}) copy-start(bf16[16,4,1024]{2,1,0:T(4,128)(2,1)} %est_ref.1) | copy-start | bytes 393220
  1.6 24.1 %all-to-all-start = ((s32[64,1,128]{2,1,0:T(1,128)}), s32[64,1,128]{2,1,0:T(1,128)S(1)}, u32[]{:S(2)}, u32[]{:S(2)}) async-start(s32[64,1,128]{2,1,0:T(1,128)} %broadcast_in_dim.6), calls=%async_computation | async-start | bytes 65536 | tf_op jit(solution)/shard_map/all_to_all | solution.py:294
  17.1 1.0 %copy-start.2 = (f32[16,4,1024]{2,1,0:T(4,128)S(1)}, f32[16,4,1024]{2,1,0:T(4,128)}, u32[]{:S(2)}) copy-start(f32[16,4,1024]{2,1,0:T(4,128)} %dat_ref.1) | copy-start | bytes 786436
  19.8 8.1 %copy-start.1 = (bf16[1024,512]{1,0:T(8,128)(2,1)S(1)}, bf16[1024,512]{1,0:T(8,128)(2,1)}, u32[]{:S(2)}) copy-start(bf16[1024,512]{1,0:T(8,128)(2,1)} %constant.14.clone.table) | copy-start | bytes 3145732
  27.9 19.9 %copy-start.3 = (f32[64,256]{1,0:T(8,128)S(1)}, f32[64,256]{1,0:T(8,128)}, u32[]{:S(2)}) copy-start(f32[64,256]{1,0:T(8,128)} %constant.16.clone.turn_ref) | copy-start | bytes 196612
  27.9 19.9 %copy-start.4 = (bf16[128,64]{1,0:T(8,128)(2,1)S(1)}, bf16[128,64]{1,0:T(8,128)(2,1)}, u32[]{:S(2)}) copy-start(bf16[128,64]{1,0:T(8,128)(2,1)} %constant.15.clone.place_ref) | copy-start | bytes 49156
  27.9 19.9 %copy-start.7 = (bf16[128,128]{1,0:T(8,128)(2,1)S(1)}, bf16[128,128]{1,0:T(8,128)(2,1)}, u32[]{:S(2)}) copy-start(bf16[128,128]{1,0:T(8,128)(2,1)} %constant.17.clone.block_ref) | copy-start | bytes 98308
  28.5 52.8 %copy-start = (bf16[1024,512]{1,0:T(8,128)(2,1)S(1)}, bf16[1024,512]{1,0:T(8,128)(2,1)}, u32[]{:S(2)}) copy-start(bf16[1024,512]{1,0:T(8,128)(2,1)} %constant.19.clone.table_ref) | copy-start | bytes 3145732
  49.1 13.6 %copy-start.6 = (bf16[128,128]{1,0:T(8,128)(2,1)S(1)}, bf16[128,128]{1,0:T(8,128)(2,1)}, u32[]{:S(2)}) copy-start(bf16[128,128]{1,0:T(8,128)(2,1)} %constant.18.clone.block_ref) | copy-start | bytes 98308

commit v6 on v5

--- a/solution.py
+++ b/solution.py
@@ -95,7 +95,7 @@
     return ((shot + 1) >> 9) & 1
 
 
-def residual_kernel(level_ref, all_lags, dat_ref, est_ref, res, part, level_out, tmp, est, lag_ref, sem):
+def residual_kernel(level_ref, all_lags, dat_ref, est_ref, res, part, level_out, est, lag_ref, sem):
     copy = pltpu.make_async_copy(all_lags.at[0], lag_ref, sem)
     copy.start()
     place = lax.axis_index("shot")
@@ -103,13 +103,11 @@
     est[...] = jnp.zeros_like(est)
     res[...] = jnp.zeros_like(res)
     part[1024:, :] = jnp.zeros((512, 128), jnp.float32)
-    tmp[...] = est_ref[...].astype(jnp.float32)
     for c in range(CHANS):
         for u in range(8):
             columns = slice(128 * u, 128 * u + 128)
-            old = tmp[:, c, columns]
-            est[pl.ds(base(2, c) + u, BLOCK, stride=CHANS * STEP), :] = old
-            res[pl.ds((CHANS + c) * 8 + u, BLOCK, stride=CHANS * 8), :] = dat_ref[:, c, columns] - old
+            est[pl.ds(base(2, c) + u, BLOCK, stride=CHANS * STEP), :] = est_ref[:, c, columns]
+            res[pl.ds((CHANS + c) * 8 + u, BLOCK, stride=CHANS * 8), :] = dat_ref[:, c, columns]
     lanes = lane_ids(8)
     copy.wait()
 
@@ -226,17 +224,18 @@
     for shift in (1, 2, 4, 8, 16, 32):
         peak = jnp.maximum(peak, pltpu.roll(peak, shift, 1))
     limit = level_ref[...] * (jnp.sqrt(peak) + 1e-6)
-    limit_ref[...] = jnp.broadcast_to(limit[None], limit_ref.shape)
+    own = lane_ids(8) == lax.broadcasted_iota(jnp.int32, (8, 128), 0)
+    limit_ref[...] = jnp.broadcast_to(jnp.sum(jnp.where(own, limit, 0.0), axis=0, keepdims=True), limit_ref.shape)
 
 
 def backward_kernel(spec_ref, limit_ref, place_ref, turn_ref, block_ref, out_ref, tmp):
-    limit = jnp.max(limit_ref[...], axis=0)
+    limit = jnp.max(limit_ref[...], axis=0, keepdims=True)
     shrunk = []
     for kk in range(8):
         value = spec_ref[64 * kk : 64 * kk + 64, :]
         square = value * value
         size = jnp.sqrt(square + swapped(square))
-        bound = limit[kk : kk + 1]
+        bound = limit[:, kk : kk + 1]
         factor = jnp.maximum(size - bound, 0.0) / jnp.maximum(size, bound)
         shrunk.append((value * factor).astype(jnp.bfloat16))
     product = jnp.dot(jnp.concatenate(shrunk, 0), block_ref[...], preferred_element_type=jnp.float32)
@@ -292,6 +291,7 @@
     own_lags = jnp.pad(jnp.concatenate([partner_lags[:, slot] for slot in range(6)]), (0, 32))
     own_lags = jnp.broadcast_to(own_lags, (DEVS, 128))
     all_lags = lax.all_to_all(own_lags, "shot", 0, 0, tiled=True)
+    old = estimate.astype(jnp.float32)
     res, part, level = call(
         residual_kernel,
         [
@@ -301,13 +301,12 @@
         ],
         [smem()] + vmem(3),
         [
-            pltpu.VMEM((BLOCK, CHANS, SAMPLES), jnp.float32),
             pltpu.VMEM((20 * CHANS * STEP + 16, 128), jnp.float32),
             pltpu.SMEM((128,), jnp.int32),
             pltpu.SemaphoreType.DMA,
         ],
         pl.CostEstimate(flops=4_000_000, bytes_accessed=16_000_000, transcendentals=0),
-    )(threshold_level, own_lags, blended, estimate)
+    )(threshold_level, own_lags, blended - old, old)
     rows = call(
         blend_kernel,
         jax.ShapeDtypeStruct((512, 512), jnp.bfloat16),
@@ -329,7 +328,7 @@
     others = lax.axis_size("chan")
     spec, limit = call(
         forward_kernel,
-        [jax.ShapeDtypeStruct((512, 128), jnp.float32), jax.ShapeDtypeStruct((others, 8, 128), jnp.float32)],
+        [jax.ShapeDtypeStruct((512, 128), jnp.float32), jax.ShapeDtypeStruct((others, 128), jnp.float32)],
         vmem(5),
         [pltpu.VMEM((512, 128), jnp.float32)],
     )(level, columns, place_table(), twiddles(), block_table(-1))

time: 82.8 us -> 82.3 us (level)
  other arithmetic: 0 us -> 1.07 us
  local copies, waits for them, and re-layouts: 2.62 us -> 1.68 us
    sub x0 -> x1, other arithmetic: none -> 1.05 us  [local(): blended - old]
    unnamed x16 -> x14, local copies, waits for them, and re-layouts: 0.99 us -> 0.05 us
  transfers between devices with their start and end apart: 1 -> 1, of which waited for: 1 -> 1; matrix products, arithmetic and copies ran while one was open for 0% -> 1% of each run, Pallas kernels for 2% -> 2%
where the time goes in v6:
time: 82.3 us; the launch traced here: 82 us
  blocking collectives  50.4 us (61%)
  starting transfers between devices  14.8 us (18%)
  Pallas kernels  7.23 us (9%)
  waiting for transfers between devices  5.94 us (7%)
  local copies, waits for them, and re-layouts  1.68 us (2%)
  other arithmetic  1.07 us (1%)
    all_to_all x1, blocking collectives, local(): lax.all_to_all(send.reshape(DEVS, 24, 128), 'shot', 0, 0, tiled=True)  19.4 us
    all_to_all x1, blocking collectives, local(): lax.all_to_all(back.reshape(DEVS, 8, 128), 'shot', 0, 0, tiled=True)  17.9 us
    all_to_all x1, starting transfers between devices, local(): all_lags = lax.all_to_all(own_lags, 'shot', 0, 0, tiled=True)  14.8 us
    all_to_all x1, blocking collectives, local(): limits = lax.all_to_all(limit, 'chan', 0, 0, tiled=True)  13.1 us
    all_to_all x1, waiting for transfers between devices, local(): all_lags = lax.all_to_all(own_lags, 'shot', 0, 0, tiled=True)  5.94 us
    pallas_call x1, Pallas kernels, local(): call(blend_kernel, jax.ShapeDtypeStruct((512, 512), jnp.bfloat16), vmem(3...  2.1 us
  transfers between devices with their start and end apart: 1, of which 1 were waited for; matrix products, arithmetic and copies ran while one was open for 1% of the time, Pallas kernels for 2%

profile of v6, /device:TPU:1, one launch (start us, length us, event | category | flops | bytes accessed | tf_op | source)
XLA Modules:
  0.0 82.0 jit_solution(11188400075704125612)
XLA Ops:
  0.0 0.9 %slice_bitcast_fusion = (s32[16]{0:T(128)S(1)}, s32[16]{0:T(128)S(1)}, s32[16]{0:T(128)S(1)}, s32[16]{0:T(128)S(1)}, s32[16]{0:T(128)S(1)}, /*index=5*/s32[16]{0:T(128)S(1)}) fusion(s32[16,6]{0,1:T(8,128)} %param.15), kind=kLoop, calls=%fused_computation.1 | loop fusion | bytes 768 | tf_op jit(solution)/shard_map/squeeze | solution.py:291
  0.9 0.1 concatenate.3
  1.0 0.6 broadcast_in_dim.6
  1.6 14.8 %all-to-all-start = ((s32[64,1,128]{2,1,0:T(1,128)}), s32[64,1,128]{2,1,0:T(1,128)S(1)}, u32[]{:S(2)}, u32[]{:S(2)}) async-start(s32[64,1,128]{2,1,0:T(1,128)} %broadcast_in_dim.6), calls=%async_computation | async-start | bytes 65536 | tf_op jit(solution)/shard_map/all_to_all | solution.py:293
  16.5 0.0 copy-start.6
  16.5 1.0 %convert_subtract_fusion = f32[8,8,1024]{2,1,0:T(8,128)S(1)} fusion(f32[8,8,1024]{2,1,0:T(8,128)} %bitcast.33, bf16[8,8,1024]{2,1,0:T(8,128)(2,1)} %bitcast.32), kind=kLoop, calls=%fused_computation | loop fusion | flops 131072 | bytes 655360 | tf_op jit(solution)/shard_map/sub | solution.py:309
  17.5 0.0 copy-done.6
  18.2 1.6 %shard_map.118 = (f32[1152,128]{1,0:T(8,128)S(1)}, f32[1536,128]{1,0:T(8,128)S(1)}, f32[8,128]{1,0:T(8,128)S(1)}) custom-call(s32[1]{0:T(128)S(6)} %copy.14.level_ref, s32[64,128]{1,0:T(8,128)S(1)} %broadcast_in_dim.5.all_lags, f32[16,4,1024]{2,1,0:T(4,128)S(1)} %bitcast.26, f32[16,4,1024]{2,1,0:T(4,128)S(1)} %convert_element_type.3.est_ref), custom_call_target="tpu_custom_call" | custom-call | flops 4000000 | bytes 16000000 | tf_op jit(solution)/shard_map/pallas_call | solution.py:295
  19.8 0.0 copy-start.1
  19.8 5.9 %all-to-all-done = s32[64,1,128]{2,1,0:T(1,128)S(1)} async-done(((s32[64,1,128]{2,1,0:T(1,128)}), s32[64,1,128]{2,1,0:T(1,128)S(1)}, u32[]{:S(2)}, u32[]{:S(2)}) %all-to-all-start) | async-done | bytes 32800 | tf_op jit(solution)/shard_map/all_to_all | solution.py:293
  25.8 2.1 %shard_map.119.rows_ref = bf16[512,512]{1,0:T(8,128)(2,1)S(1)} custom-call(s32[64,128]{1,0:T(8,128)S(1)} %bitcast.29, f32[1152,128]{1,0:T(8,128)S(1)} %get-tuple-element.11.res_ref, f32[1536,128]{1,0:T(8,128)S(1)} %get-tuple-element.12.part), custom_call_target="tpu_custom_call" | custom-call | tf_op jit(solution)/shard_map/pallas_call | solution.py:310
  27.9 0.0 copy-done.1
  27.9 0.0 copy-start.2
  27.9 0.0 copy-start.3
  27.9 0.0 copy-start.5
  27.9 0.5 shard_map.120
  28.5 0.0 copy-start
  28.5 19.4 %all_to_all.29 = bf16[64,24,128]{2,1,0:T(8,128)(2,1)S(1)} all-to-all(bf16[64,24,128]{2,1,0:T(8,128)(2,1)S(1)} %bitcast.25), channel_id=1, replica_groups=mesh['shot'=64,'chan'=8] {'shot'}, dimensions={0} | all-to-all | bytes 786432 | tf_op jit(solution)/shard_map/all_to_all | solution.py:327
  47.8 0.0 copy-done.2
  47.9 0.0 copy-done.3
  47.9 0.0 copy-done.5
  47.9 0.0 copy-start.4
  47.9 1.3 %shard_map.121 = (f32[512,128]{1,0:T(8,128)S(1)}, f32[8,128]{1,0:T(8,128)S(1)}) custom-call(f32[8,128]{1,0:T(8,128)S(1)} %get-tuple-element.10.level_ref, bf16[1536,128]{1,0:T(8,128)(2,1)S(1)} %bitcast.24, bf16[128,64]{1,0:T(8,128)(2,1)S(1)} %copy-done.3, f32[64,256]{1,0:T(8,128)S(1)} %copy-done.2, bf16[128,128]{1,0:T(8,128)(2,1)S(1)} %copy-done.5), custom_call_target="tpu_custom_call" | custom-call | tf_op jit(solution)/shard_map/pallas_call | solution.py:329
  49.1 13.1 %all_to_all.30 = f32[8,1,128]{2,1,0:T(1,128)S(1)} all-to-all(f32[8,1,128]{2,1,0:T(1,128)S(1)} %bitcast.31), channel_id=1, replica_groups=mesh['shot'=64,'chan'=8] {'chan'}, dimensions={0} | all-to-all | bytes 8192 | tf_op jit(solution)/shard_map/all_to_all | solution.py:335
  62.3 0.0 copy-done.4
  62.3 0.7 shard_map.122
  63.0 17.9 %all_to_all.31 = bf16[64,8,128]{2,1,0:T(8,128)(2,1)S(1)} all-to-all(bf16[64,8,128]{2,1,0:T(8,128)(2,1)S(1)} %bitcast.27), channel_id=1, replica_groups=mesh['shot'=64,'chan'=8] {'shot'}, dimensions={0} | all-to-all | bytes 262144 | tf_op jit(solution)/shard_map/all_to_all | solution.py:342
  80.9 0.0 copy-done
  80.9 1.1 %shard_map.123 = f32[16,4,1024]{2,1,0:T(4,128)} custom-call(bf16[512,128]{1,0:T(8,128)(2,1)S(1)} %bitcast.28, bf16[1024,512]{1,0:T(8,128)(2,1)S(1)} %copy-done), custom_call_target="tpu_custom_call" | custom-call | tf_op jit(solution)/shard_map/pallas_call | solution.py:343
  (3 shorter events, 0.0 us)
Async XLA Ops:
  1.6 24.1 %all-to-all-start = ((s32[64,1,128]{2,1,0:T(1,128)}), s32[64,1,128]{2,1,0:T(1,128)S(1)}, u32[]{:S(2)}, u32[]{:S(2)}) async-start(s32[64,1,128]{2,1,0:T(1,128)} %broadcast_in_dim.6), calls=%async_computation | async-start | bytes 65536 | tf_op jit(solution)/shard_map/all_to_all | solution.py:293
  16.5 1.1 %copy-start.6 = (bf16[16,4,1024]{2,1,0:T(4,128)(2,1)S(1)}, bf16[16,4,1024]{2,1,0:T(4,128)(2,1)}, u32[]{:S(2)}) copy-start(bf16[16,4,1024]{2,1,0:T(4,128)(2,1)} %param.14) | copy-start | bytes 393220
  19.8 8.1 %copy-start.1 = (bf16[1024,512]{1,0:T(8,128)(2,1)S(1)}, bf16[1024,512]{1,0:T(8,128)(2,1)}, u32[]{:S(2)}) copy-start(bf16[1024,512]{1,0:T(8,128)(2,1)} %constant.14.clone.table) | copy-start | bytes 3145732
  27.9 20.0 %copy-start.2 = (f32[64,256]{1,0:T(8,128)S(1)}, f32[64,256]{1,0:T(8,128)}, u32[]{:S(2)}) copy-start(f32[64,256]{1,0:T(8,128)} %constant.16.clone.turn_ref) | copy-start | bytes 196612
  27.9 19.9 %copy-start.3 = (bf16[128,64]{1,0:T(8,128)(2,1)S(1)}, bf16[128,64]{1,0:T(8,128)(2,1)}, u32[]{:S(2)}) copy-start(bf16[128,64]{1,0:T(8,128)(2,1)} %constant.15.clone.place_ref) | copy-start | bytes 49156
  27.9 19.9 %copy-start.5 = (bf16[128,128]{1,0:T(8,128)(2,1)S(1)}, bf16[128,128]{1,0:T(8,128)(2,1)}, u32[]{:S(2)}) copy-start(bf16[128,128]{1,0:T(8,128)(2,1)} %constant.17.clone.block_ref) | copy-start | bytes 98308
  28.5 52.4 %copy-start = (bf16[1024,512]{1,0:T(8,128)(2,1)S(1)}, bf16[1024,512]{1,0:T(8,128)(2,1)}, u32[]{:S(2)}) copy-start(bf16[1024,512]{1,0:T(8,128)(2,1)} %constant.19.clone.table_ref) | copy-start | bytes 3145732
  47.9 14.4 %copy-start.4 = (bf16[128,128]{1,0:T(8,128)(2,1)S(1)}, bf16[128,128]{1,0:T(8,128)(2,1)}, u32[]{:S(2)}) copy-start(bf16[128,128]{1,0:T(8,128)(2,1)} %constant.18.clone.block_ref) | copy-start | bytes 98308

commit v7 on v6

--- a/solution.py
+++ b/solution.py
@@ -149,19 +149,26 @@
     for copy in copies:
         copy.wait()
 
-    @pl.loop(0, BLOCK + 4, unroll=5)
-    def _(step):
-        n = step - 2
+    def add_row(n, steps):
         for side in range(2):
             shot = (512 * side + BLOCK * place + n + SHOTS) & (SHOTS - 1)
             fleet = fleet_of(shot)
             total = [None] * CHANS
             for flip, ahead in ((0, -1), (0, 1), (1, -1), (1, 0), (1, 1)):
+                if ahead not in steps:
+                    continue
                 lag = lag_ref[side * 3 + ((n + BLOCK) >> 4), (3 * (fleet ^ flip) + 1 + ahead) * BLOCK + (shot & 15)]
                 add_shifted(total, res, base(res_row(side ^ flip, n + ahead), 0), lag, lanes)
             for c in range(CHANS):
                 rows = pl.ds((place_of(side, n) + c * BLOCK) * 8, 8)
                 upd[rows, :] = part[rows, :] + 0.25 * total[c]
+
+    for n, steps in ((-2, (1,)), (-1, (0, 1)), (BLOCK, (-1, 0)), (BLOCK + 1, (-1,))):
+        add_row(n, steps)
+
+    @pl.loop(0, BLOCK, unroll=4)
+    def _(n):
+        add_row(n, (-1, 0, 1))
 
     octaves = [upd[pl.ds(u, 256, stride=8), :] for u in range(8)]
     for parity in range(2):

time: 82.3 us -> 82.3 us (level)
  no operation moved by 1% of the time
where the time goes in v7:
time: 82.3 us; the launch traced here: 82 us
  blocking collectives  50.4 us (61%)
  starting transfers between devices  14.8 us (18%)
  Pallas kernels  7.25 us (9%)
  waiting for transfers between devices  5.94 us (7%)
  local copies, waits for them, and re-layouts  1.68 us (2%)
  other arithmetic  1.07 us (1%)
    all_to_all x1, blocking collectives, local(): lax.all_to_all(send.reshape(DEVS, 24, 128), 'shot', 0, 0, tiled=True)  19.4 us
    all_to_all x1, blocking collectives, local(): lax.all_to_all(back.reshape(DEVS, 8, 128), 'shot', 0, 0, tiled=True)  17.9 us
    all_to_all x1, starting transfers between devices, local(): all_lags = lax.all_to_all(own_lags, 'shot', 0, 0, tiled=True)  14.8 us
    all_to_all x1, blocking collectives, local(): limits = lax.all_to_all(limit, 'chan', 0, 0, tiled=True)  13.1 us
    all_to_all x1, waiting for transfers between devices, local(): all_lags = lax.all_to_all(own_lags, 'shot', 0, 0, tiled=True)  5.94 us
    pallas_call x1, Pallas kernels, local(): call(blend_kernel, jax.ShapeDtypeStruct((512, 512), jnp.bfloat16), vmem(3...  2.12 us
  transfers between devices with their start and end apart: 1, of which 1 were waited for; matrix products, arithmetic and copies ran while one was open for 1% of the time, Pallas kernels for 2%

profile of v7, /device:TPU:1, one launch (start us, length us, event | category | flops | bytes accessed | tf_op | source)
XLA Modules:
  0.0 82.0 jit_solution(366749680769514632)
XLA Ops:
  0.0 0.9 %slice_bitcast_fusion = (s32[16]{0:T(128)S(1)}, s32[16]{0:T(128)S(1)}, s32[16]{0:T(128)S(1)}, s32[16]{0:T(128)S(1)}, s32[16]{0:T(128)S(1)}, /*index=5*/s32[16]{0:T(128)S(1)}) fusion(s32[16,6]{0,1:T(8,128)} %param.15), kind=kLoop, calls=%fused_computation.1 | loop fusion | bytes 768 | tf_op jit(solution)/shard_map/squeeze | solution.py:298
  0.9 0.1 concatenate.3
  1.0 0.6 broadcast_in_dim.6
  1.6 14.8 %all-to-all-start = ((s32[64,1,128]{2,1,0:T(1,128)}), s32[64,1,128]{2,1,0:T(1,128)S(1)}, u32[]{:S(2)}, u32[]{:S(2)}) async-start(s32[64,1,128]{2,1,0:T(1,128)} %broadcast_in_dim.6), calls=%async_computation | async-start | bytes 65536 | tf_op jit(solution)/shard_map/all_to_all | solution.py:300
  16.5 0.0 copy-start.6
  16.5 1.0 %convert_subtract_fusion = f32[8,8,1024]{2,1,0:T(8,128)S(1)} fusion(f32[8,8,1024]{2,1,0:T(8,128)} %bitcast.33, bf16[8,8,1024]{2,1,0:T(8,128)(2,1)} %bitcast.32), kind=kLoop, calls=%fused_computation | loop fusion | flops 131072 | bytes 655360 | tf_op jit(solution)/shard_map/sub | solution.py:316
  17.5 0.0 copy-done.6
  18.2 1.6 %shard_map.118 = (f32[1152,128]{1,0:T(8,128)S(1)}, f32[1536,128]{1,0:T(8,128)S(1)}, f32[8,128]{1,0:T(8,128)S(1)}) custom-call(s32[1]{0:T(128)S(6)} %copy.14.level_ref, s32[64,128]{1,0:T(8,128)S(1)} %broadcast_in_dim.5.all_lags, f32[16,4,1024]{2,1,0:T(4,128)S(1)} %bitcast.26, f32[16,4,1024]{2,1,0:T(4,128)S(1)} %convert_element_type.3.est_ref), custom_call_target="tpu_custom_call" | custom-call | flops 4000000 | bytes 16000000 | tf_op jit(solution)/shard_map/pallas_call | solution.py:302
  19.8 0.0 copy-start.1
  19.8 5.9 %all-to-all-done = s32[64,1,128]{2,1,0:T(1,128)S(1)} async-done(((s32[64,1,128]{2,1,0:T(1,128)}), s32[64,1,128]{2,1,0:T(1,128)S(1)}, u32[]{:S(2)}, u32[]{:S(2)}) %all-to-all-start) | async-done | bytes 32800 | tf_op jit(solution)/shard_map/all_to_all | solution.py:300
  25.8 2.1 %shard_map.119.rows_ref = bf16[512,512]{1,0:T(8,128)(2,1)S(1)} custom-call(s32[64,128]{1,0:T(8,128)S(1)} %bitcast.29, f32[1152,128]{1,0:T(8,128)S(1)} %get-tuple-element.11.res_ref, f32[1536,128]{1,0:T(8,128)S(1)} %get-tuple-element.12.part), custom_call_target="tpu_custom_call" | custom-call | tf_op jit(solution)/shard_map/pallas_call | solution.py:317
  27.9 0.0 copy-done.1
  27.9 0.0 copy-start.2
  27.9 0.0 copy-start.3
  27.9 0.0 copy-start.5
  28.0 0.5 shard_map.120
  28.5 0.0 copy-start
  28.5 19.4 %all_to_all.29 = bf16[64,24,128]{2,1,0:T(8,128)(2,1)S(1)} all-to-all(bf16[64,24,128]{2,1,0:T(8,128)(2,1)S(1)} %bitcast.25), channel_id=1, replica_groups=mesh['shot'=64,'chan'=8] {'shot'}, dimensions={0} | all-to-all | bytes 786432 | tf_op jit(solution)/shard_map/all_to_all | solution.py:334
  47.9 0.0 copy-done.2
  47.9 0.0 copy-done.3
  47.9 0.0 copy-done.5
  47.9 0.0 copy-start.4
  47.9 1.3 %shard_map.121 = (f32[512,128]{1,0:T(8,128)S(1)}, f32[8,128]{1,0:T(8,128)S(1)}) custom-call(f32[8,128]{1,0:T(8,128)S(1)} %get-tuple-element.10.level_ref, bf16[1536,128]{1,0:T(8,128)(2,1)S(1)} %bitcast.24, bf16[128,64]{1,0:T(8,128)(2,1)S(1)} %copy-done.3, f32[64,256]{1,0:T(8,128)S(1)} %copy-done.2, bf16[128,128]{1,0:T(8,128)(2,1)S(1)} %copy-done.5), custom_call_target="tpu_custom_call" | custom-call | tf_op jit(solution)/shard_map/pallas_call | solution.py:336
  49.2 13.1 %all_to_all.30 = f32[8,1,128]{2,1,0:T(1,128)S(1)} all-to-all(f32[8,1,128]{2,1,0:T(1,128)S(1)} %bitcast.31), channel_id=1, replica_groups=mesh['shot'=64,'chan'=8] {'chan'}, dimensions={0} | all-to-all | bytes 8192 | tf_op jit(solution)/shard_map/all_to_all | solution.py:342
  62.3 0.0 copy-done.4
  62.3 0.7 shard_map.122
  63.0 17.9 %all_to_all.31 = bf16[64,8,128]{2,1,0:T(8,128)(2,1)S(1)} all-to-all(bf16[64,8,128]{2,1,0:T(8,128)(2,1)S(1)} %bitcast.27), channel_id=1, replica_groups=mesh['shot'=64,'chan'=8] {'shot'}, dimensions={0} | all-to-all | bytes 262144 | tf_op jit(solution)/shard_map/all_to_all | solution.py:349
  80.9 0.0 copy-done
  80.9 1.1 %shard_map.123 = f32[16,4,1024]{2,1,0:T(4,128)} custom-call(bf16[512,128]{1,0:T(8,128)(2,1)S(1)} %bitcast.28, bf16[1024,512]{1,0:T(8,128)(2,1)S(1)} %copy-done), custom_call_target="tpu_custom_call" | custom-call | tf_op jit(solution)/shard_map/pallas_call | solution.py:350
  (3 shorter events, 0.0 us)
Async XLA Ops:
  1.6 24.1 %all-to-all-start = ((s32[64,1,128]{2,1,0:T(1,128)}), s32[64,1,128]{2,1,0:T(1,128)S(1)}, u32[]{:S(2)}, u32[]{:S(2)}) async-start(s32[64,1,128]{2,1,0:T(1,128)} %broadcast_in_dim.6), calls=%async_computation | async-start | bytes 65536 | tf_op jit(solution)/shard_map/all_to_all | solution.py:300
  16.5 1.1 %copy-start.6 = (bf16[16,4,1024]{2,1,0:T(4,128)(2,1)S(1)}, bf16[16,4,1024]{2,1,0:T(4,128)(2,1)}, u32[]{:S(2)}) copy-start(bf16[16,4,1024]{2,1,0:T(4,128)(2,1)} %param.14) | copy-start | bytes 393220
  19.8 8.1 %copy-start.1 = (bf16[1024,512]{1,0:T(8,128)(2,1)S(1)}, bf16[1024,512]{1,0:T(8,128)(2,1)}, u32[]{:S(2)}) copy-start(bf16[1024,512]{1,0:T(8,128)(2,1)} %constant.14.clone.table) | copy-start | bytes 3145732
  27.9 20.0 %copy-start.2 = (f32[64,256]{1,0:T(8,128)S(1)}, f32[64,256]{1,0:T(8,128)}, u32[]{:S(2)}) copy-start(f32[64,256]{1,0:T(8,128)} %constant.16.clone.turn_ref) | copy-start | bytes 196612
  27.9 19.9 %copy-start.3 = (bf16[128,64]{1,0:T(8,128)(2,1)S(1)}, bf16[128,64]{1,0:T(8,128)(2,1)}, u32[]{:S(2)}) copy-start(bf16[128,64]{1,0:T(8,128)(2,1)} %constant.15.clone.place_ref) | copy-start | bytes 49156
  27.9 19.9 %copy-start.5 = (bf16[128,128]{1,0:T(8,128)(2,1)S(1)}, bf16[128,128]{1,0:T(8,128)(2,1)}, u32[]{:S(2)}) copy-start(bf16[128,128]{1,0:T(8,128)(2,1)} %constant.17.clone.block_ref) | copy-start | bytes 98308
  28.5 52.4 %copy-start = (bf16[1024,512]{1,0:T(8,128)(2,1)S(1)}, bf16[1024,512]{1,0:T(8,128)(2,1)}, u32[]{:S(2)}) copy-start(bf16[1024,512]{1,0:T(8,128)(2,1)} %constant.19.clone.table_ref) | copy-start | bytes 3145732
  47.9 14.4 %copy-start.4 = (bf16[128,128]{1,0:T(8,128)(2,1)S(1)}, bf16[128,128]{1,0:T(8,128)(2,1)}, u32[]{:S(2)}) copy-start(bf16[128,128]{1,0:T(8,128)(2,1)} %constant.18.clone.block_ref) | copy-start | bytes 98308

commit v8 on v6

--- a/solution.py
+++ b/solution.py
@@ -111,7 +111,7 @@
     lanes = lane_ids(8)
     copy.wait()
 
-    @pl.loop(0, BLOCK + 2, unroll=3)
+    @pl.loop(0, BLOCK + 2, unroll=6)
     def _(step):
         n = step - 1
         for side in range(2):
@@ -149,7 +149,7 @@
     for copy in copies:
         copy.wait()
 
-    @pl.loop(0, BLOCK + 4, unroll=5)
+    @pl.loop(0, BLOCK + 4, unroll=10)
     def _(step):
         n = step - 2
         for side in range(2):

time: 82.3 us -> 82 us (level)
  no operation moved by 1% of the time
where the time goes in v8:
time: 82 us; the launch traced here: 81.7 us
  blocking collectives  50.3 us (61%)
  starting transfers between devices  14.8 us (18%)
  Pallas kernels  6.95 us (8%)
  waiting for transfers between devices  6.1 us (7%)
  local copies, waits for them, and re-layouts  1.68 us (2%)
  other arithmetic  1.07 us (1%)
    all_to_all x1, blocking collectives, local(): lax.all_to_all(send.reshape(DEVS, 24, 128), 'shot', 0, 0, tiled=True)  19.2 us
    all_to_all x1, blocking collectives, local(): lax.all_to_all(back.reshape(DEVS, 8, 128), 'shot', 0, 0, tiled=True)  17.9 us
    all_to_all x1, starting transfers between devices, local(): all_lags = lax.all_to_all(own_lags, 'shot', 0, 0, tiled=True)  14.8 us
    all_to_all x1, blocking collectives, local(): limits = lax.all_to_all(limit, 'chan', 0, 0, tiled=True)  13.1 us
    all_to_all x1, waiting for transfers between devices, local(): all_lags = lax.all_to_all(own_lags, 'shot', 0, 0, tiled=True)  6.1 us
    pallas_call x1, Pallas kernels, local(): call(blend_kernel, jax.ShapeDtypeStruct((512, 512), jnp.bfloat16), vmem(3...  1.98 us
  transfers between devices with their start and end apart: 1, of which 1 were waited for; matrix products, arithmetic and copies ran while one was open for 1% of the time, Pallas kernels for 2%

profile of v8, /device:TPU:1, one launch (start us, length us, event | category | flops | bytes accessed | tf_op | source)
XLA Modules:
  0.0 81.7 jit_solution(5527644836543512730)
XLA Ops:
  0.0 0.9 %slice_bitcast_fusion = (s32[16]{0:T(128)S(1)}, s32[16]{0:T(128)S(1)}, s32[16]{0:T(128)S(1)}, s32[16]{0:T(128)S(1)}, s32[16]{0:T(128)S(1)}, /*index=5*/s32[16]{0:T(128)S(1)}) fusion(s32[16,6]{0,1:T(8,128)} %param.15), kind=kLoop, calls=%fused_computation.1 | loop fusion | bytes 768 | tf_op jit(solution)/shard_map/squeeze | solution.py:291
  0.9 0.1 concatenate.3
  1.0 0.6 broadcast_in_dim.6
  1.6 14.8 %all-to-all-start = ((s32[64,1,128]{2,1,0:T(1,128)}), s32[64,1,128]{2,1,0:T(1,128)S(1)}, u32[]{:S(2)}, u32[]{:S(2)}) async-start(s32[64,1,128]{2,1,0:T(1,128)} %broadcast_in_dim.6), calls=%async_computation | async-start | bytes 65536 | tf_op jit(solution)/shard_map/all_to_all | solution.py:293
  16.5 0.0 copy-start.6
  16.5 1.0 %convert_subtract_fusion = f32[8,8,1024]{2,1,0:T(8,128)S(1)} fusion(f32[8,8,1024]{2,1,0:T(8,128)} %bitcast.33, bf16[8,8,1024]{2,1,0:T(8,128)(2,1)} %bitcast.32), kind=kLoop, calls=%fused_computation | loop fusion | flops 131072 | bytes 655360 | tf_op jit(solution)/shard_map/sub | solution.py:309
  17.5 0.0 copy-done.6
  18.2 1.4 %shard_map.118 = (f32[1152,128]{1,0:T(8,128)S(1)}, f32[1536,128]{1,0:T(8,128)S(1)}, f32[8,128]{1,0:T(8,128)S(1)}) custom-call(s32[1]{0:T(128)S(6)} %copy.14.level_ref, s32[64,128]{1,0:T(8,128)S(1)} %broadcast_in_dim.5.all_lags, f32[16,4,1024]{2,1,0:T(4,128)S(1)} %bitcast.26, f32[16,4,1024]{2,1,0:T(4,128)S(1)} %convert_element_type.3.est_ref), custom_call_target="tpu_custom_call" | custom-call | flops 4000000 | bytes 16000000 | tf_op jit(solution)/shard_map/pallas_call | solution.py:295
  19.7 0.0 copy-start.1
  19.7 6.1 %all-to-all-done = s32[64,1,128]{2,1,0:T(1,128)S(1)} async-done(((s32[64,1,128]{2,1,0:T(1,128)}), s32[64,1,128]{2,1,0:T(1,128)S(1)}, u32[]{:S(2)}, u32[]{:S(2)}) %all-to-all-start) | async-done | bytes 32800 | tf_op jit(solution)/shard_map/all_to_all | solution.py:293
  25.8 2.0 %shard_map.119.rows_ref = bf16[512,512]{1,0:T(8,128)(2,1)S(1)} custom-call(s32[64,128]{1,0:T(8,128)S(1)} %bitcast.29, f32[1152,128]{1,0:T(8,128)S(1)} %get-tuple-element.11.res_ref, f32[1536,128]{1,0:T(8,128)S(1)} %get-tuple-element.12.part), custom_call_target="tpu_custom_call" | custom-call | tf_op jit(solution)/shard_map/pallas_call | solution.py:310
  27.8 0.0 copy-done.1
  27.8 0.0 copy-start.2
  27.8 0.0 copy-start.3
  27.8 0.0 copy-start.5
  27.8 0.5 shard_map.120
  28.4 0.0 copy-start
  28.4 19.2 %all_to_all.29 = bf16[64,24,128]{2,1,0:T(8,128)(2,1)S(1)} all-to-all(bf16[64,24,128]{2,1,0:T(8,128)(2,1)S(1)} %bitcast.25), channel_id=1, replica_groups=mesh['shot'=64,'chan'=8] {'shot'}, dimensions={0} | all-to-all | bytes 786432 | tf_op jit(solution)/shard_map/all_to_all | solution.py:327
  47.6 0.0 copy-done.2
  47.6 0.0 copy-done.3
  47.6 0.0 copy-done.5
  47.6 0.0 copy-start.4
  47.6 1.3 %shard_map.121 = (f32[512,128]{1,0:T(8,128)S(1)}, f32[8,128]{1,0:T(8,128)S(1)}) custom-call(f32[8,128]{1,0:T(8,128)S(1)} %get-tuple-element.10.level_ref, bf16[1536,128]{1,0:T(8,128)(2,1)S(1)} %bitcast.24, bf16[128,64]{1,0:T(8,128)(2,1)S(1)} %copy-done.3, f32[64,256]{1,0:T(8,128)S(1)} %copy-done.2, bf16[128,128]{1,0:T(8,128)(2,1)S(1)} %copy-done.5), custom_call_target="tpu_custom_call" | custom-call | tf_op jit(solution)/shard_map/pallas_call | solution.py:329
  48.9 13.1 %all_to_all.30 = f32[8,1,128]{2,1,0:T(1,128)S(1)} all-to-all(f32[8,1,128]{2,1,0:T(1,128)S(1)} %bitcast.31), channel_id=1, replica_groups=mesh['shot'=64,'chan'=8] {'chan'}, dimensions={0} | all-to-all | bytes 8192 | tf_op jit(solution)/shard_map/all_to_all | solution.py:335
  62.0 0.0 copy-done.4
  62.0 0.7 shard_map.122
  62.7 17.9 %all_to_all.31 = bf16[64,8,128]{2,1,0:T(8,128)(2,1)S(1)} all-to-all(bf16[64,8,128]{2,1,0:T(8,128)(2,1)S(1)} %bitcast.27), channel_id=1, replica_groups=mesh['shot'=64,'chan'=8] {'shot'}, dimensions={0} | all-to-all | bytes 262144 | tf_op jit(solution)/shard_map/all_to_all | solution.py:342
  80.6 0.0 copy-done
  80.6 1.1 %shard_map.123 = f32[16,4,1024]{2,1,0:T(4,128)} custom-call(bf16[512,128]{1,0:T(8,128)(2,1)S(1)} %bitcast.28, bf16[1024,512]{1,0:T(8,128)(2,1)S(1)} %copy-done), custom_call_target="tpu_custom_call" | custom-call | tf_op jit(solution)/shard_map/pallas_call | solution.py:343
  (3 shorter events, 0.0 us)
Async XLA Ops:
  1.6 24.1 %all-to-all-start = ((s32[64,1,128]{2,1,0:T(1,128)}), s32[64,1,128]{2,1,0:T(1,128)S(1)}, u32[]{:S(2)}, u32[]{:S(2)}) async-start(s32[64,1,128]{2,1,0:T(1,128)} %broadcast_in_dim.6), calls=%async_computation | async-start | bytes 65536 | tf_op jit(solution)/shard_map/all_to_all | solution.py:293
  16.5 1.1 %copy-start.6 = (bf16[16,4,1024]{2,1,0:T(4,128)(2,1)S(1)}, bf16[16,4,1024]{2,1,0:T(4,128)(2,1)}, u32[]{:S(2)}) copy-start(bf16[16,4,1024]{2,1,0:T(4,128)(2,1)} %param.14) | copy-start | bytes 393220
  19.7 8.1 %copy-start.1 = (bf16[1024,512]{1,0:T(8,128)(2,1)S(1)}, bf16[1024,512]{1,0:T(8,128)(2,1)}, u32[]{:S(2)}) copy-start(bf16[1024,512]{1,0:T(8,128)(2,1)} %constant.14.clone.table) | copy-start | bytes 3145732
  27.8 19.8 %copy-start.2 = (f32[64,256]{1,0:T(8,128)S(1)}, f32[64,256]{1,0:T(8,128)}, u32[]{:S(2)}) copy-start(f32[64,256]{1,0:T(8,128)} %constant.16.clone.turn_ref) | copy-start | bytes 196612
  27.8 19.8 %copy-start.3 = (bf16[128,64]{1,0:T(8,128)(2,1)S(1)}, bf16[128,64]{1,0:T(8,128)(2,1)}, u32[]{:S(2)}) copy-start(bf16[128,64]{1,0:T(8,128)(2,1)} %constant.15.clone.place_ref) | copy-start | bytes 49156
  27.8 19.8 %copy-start.5 = (bf16[128,128]{1,0:T(8,128)(2,1)S(1)}, bf16[128,128]{1,0:T(8,128)(2,1)}, u32[]{:S(2)}) copy-start(bf16[128,128]{1,0:T(8,128)(2,1)} %constant.17.clone.block_ref) | copy-start | bytes 98308
  28.4 52.3 %copy-start = (bf16[1024,512]{1,0:T(8,128)(2,1)S(1)}, bf16[1024,512]{1,0:T(8,128)(2,1)}, u32[]{:S(2)}) copy-start(bf16[1024,512]{1,0:T(8,128)(2,1)} %constant.19.clone.table_ref) | copy-start | bytes 3145732
  47.6 14.4 %copy-start.4 = (bf16[128,128]{1,0:T(8,128)(2,1)S(1)}, bf16[128,128]{1,0:T(8,128)(2,1)}, u32[]{:S(2)}) copy-start(bf16[128,128]{1,0:T(8,128)(2,1)} %constant.18.clone.block_ref) | copy-start | bytes 98308
